TPU v7x, 512 devices: a whole 4x8x8 slice. The times are simulated.
512 devices in a mesh: dap: 128 (over x, y, z_hi, core), rep: 4 (over z_lo).
Axes of the slice: x: 4, y: 8, z: 8 (z_hi: 2, z_lo: 4; z = z_hi * 4 + z_lo), core: 2. Of those that a mesh axis runs over, the one named last changes fastest.
Arguments:
- alignment_source_tensor: float32 [256, 512, 256], P('dap'), may hold values from -6 to 6
- couple_source_tensor: float32 [512, 512, 128], P('dap', 'rep'), may hold values from -6 to 6
- horizontal_scale_factor: float32 [256], replicated, may hold values from 0.3 to 3
- horizontal_projection_matrix: bfloat16 [256, 1024], replicated, may hold values from -12 to 12
- couple_scale_factor: float32 [128], replicated, may hold values from 0.3 to 3
- couple_offset_matrix: bfloat16 [128, 8], replicated, may hold values from -0.5 to 0.5
- horizontal_final_matrix: bfloat16 [256, 256], replicated, may hold values from -1.5 to 1.5
- vertical_scale_factor: float32 [256], replicated, may hold values from 0.3 to 3
- vertical_projection_matrix: bfloat16 [256, 1024], replicated, may hold values from -12 to 12
- vertical_final_matrix: bfloat16 [256, 256], replicated, may hold values from -1.5 to 1.5
- tensorial_scale_factor: float32 [256], replicated, may hold values from 0.3 to 3
- tensorial_factor_matrix: bfloat16 [256, 64], replicated, may hold values from -0.375 to 0.375
- tensorial_final_matrix: bfloat16 [1024, 128], replicated, may hold values from -1 to 1
Outputs:
- alignment_target_tensor: float32 [256, 512, 256], P(None, 'dap')
- couple_target_tensor: float32 [512, 512, 128], P('dap', 'rep')
All inputs are finite; a program needn't handle non-finite values.
Results may differ from a plain program's by a relative error of at most 0.02.
Values may be sent and summed in bfloat16 or wider, within the bound.
A program may use at most 64 MiB of HBM per device.

v0:
```python
import jax
import jax.numpy as jnp
from jax import lax
from jax.sharding import PartitionSpec as P

HEADS = 8
HEAD_DIM = 32


def standardize_features(inputs, norm_gain):
    average = jnp.mean(inputs, axis=-1, keepdims=True)
    centred = inputs - average
    variance = jnp.mean(centred * centred, axis=-1, keepdims=True)
    return centred * lax.rsqrt(variance + 1e-05) * norm_gain


def attend(queries_in, keys_in, values_in, gates_in, bias_heads):
    q_len = queries_in.shape[0]
    k_len = keys_in.shape[0]
    queries = queries_in.reshape(q_len, HEADS, HEAD_DIM)
    key_heads = keys_in.reshape(k_len, HEADS, HEAD_DIM)
    value_heads = values_in.reshape(k_len, HEADS, HEAD_DIM)
    logits = jnp.einsum(
        "qhd,khd->hqk", queries, key_heads, preferred_element_type=jnp.float32
    ) * HEAD_DIM ** (-0.5)
    logits = logits + bias_heads.astype(jnp.float32)
    maximum = jnp.max(logits, axis=-1, keepdims=True)
    exponent = jnp.exp(logits - maximum)
    weights = (exponent / jnp.sum(exponent, axis=-1, keepdims=True)).astype(jnp.bfloat16)
    attended = jnp.einsum(
        "hqk,khd->qhd", weights, value_heads, preferred_element_type=jnp.float32
    ).reshape(q_len, HEADS * HEAD_DIM)
    return (attended * jax.nn.sigmoid(gates_in.astype(jnp.float32))).astype(jnp.bfloat16)


def column_attention(vertical_result):
    rows_all = vertical_result.shape[0]
    local_res = vertical_result.shape[1]
    feature_width = HEADS * HEAD_DIM
    queries = vertical_result[..., :feature_width].reshape(rows_all, local_res, HEADS, HEAD_DIM)
    key_heads = vertical_result[..., feature_width : 2 * feature_width].reshape(
        rows_all, local_res, HEADS, HEAD_DIM
    )
    value_heads = vertical_result[..., 2 * feature_width : 3 * feature_width].reshape(
        rows_all, local_res, HEADS, HEAD_DIM
    )
    gates_in = vertical_result[..., 3 * feature_width :]
    logits = jnp.einsum(
        "sbhd,tbhd->bhst", queries, key_heads, preferred_element_type=jnp.float32
    ) * HEAD_DIM ** (-0.5)
    maximum = jnp.max(logits, axis=-1, keepdims=True)
    exponent = jnp.exp(logits - maximum)
    weights = (exponent / jnp.sum(exponent, axis=-1, keepdims=True)).astype(jnp.bfloat16)
    attended = jnp.einsum(
        "bhst,tbhd->sbhd", weights, value_heads, preferred_element_type=jnp.float32
    ).reshape(rows_all, local_res, feature_width)
    return (attended * jax.nn.sigmoid(gates_in.astype(jnp.float32))).astype(jnp.bfloat16)


def vertical_softmax_mixing(
    amino_number, vertical_scale_factor, vertical_projection_matrix, vertical_final_matrix
):
    vertical_standardized = standardize_features(amino_number, vertical_scale_factor).astype(
        jnp.bfloat16
    )
    vertical_result = jnp.dot(
        vertical_standardized, vertical_projection_matrix, preferred_element_type=jnp.float32
    ).astype(jnp.bfloat16)
    vertical_sigmoid_masked = column_attention(vertical_result)
    return amino_number + jnp.dot(
        vertical_sigmoid_masked, vertical_final_matrix, preferred_element_type=jnp.float32
    )


def shards(
    alignment_source_tensor,
    couple_source_tensor,
    horizontal_scale_factor,
    horizontal_projection_matrix,
    couple_scale_factor,
    couple_offset_matrix,
    horizontal_final_matrix,
    vertical_scale_factor,
    vertical_projection_matrix,
    vertical_final_matrix,
    tensorial_scale_factor,
    tensorial_factor_matrix,
    tensorial_final_matrix,
):
    feature_width = alignment_source_tensor.shape[2]
    chain_extent = alignment_source_tensor.shape[1]
    rep_count = lax.axis_size("rep")
    rep_index = lax.axis_index("rep")
    ln_pair = standardize_features(couple_source_tensor, couple_scale_factor).astype(jnp.bfloat16)
    local_bias = jnp.einsum(
        "ijc,ch->hij", ln_pair, couple_offset_matrix, preferred_element_type=jnp.float32
    ).astype(jnp.bfloat16)
    rows_bias = lax.all_gather(local_bias, "dap", axis=1, tiled=True)
    horizontal_standardized = standardize_features(
        alignment_source_tensor, horizontal_scale_factor
    ).astype(jnp.bfloat16)
    full_bias = lax.all_gather(rows_bias, "rep", axis=2, tiled=True)
    horizontal_result = jnp.dot(
        horizontal_standardized, horizontal_projection_matrix, preferred_element_type=jnp.float32
    ).astype(jnp.bfloat16)

    def row_whole(projected):
        return attend(
            projected[:, :feature_width],
            projected[:, feature_width : 2 * feature_width],
            projected[:, 2 * feature_width : 3 * feature_width],
            projected[:, 3 * feature_width :],
            full_bias,
        )

    horizontal_sigmoid_masked = lax.map(row_whole, horizontal_result)
    alignment_intermediate = alignment_source_tensor + jnp.dot(
        horizontal_sigmoid_masked, horizontal_final_matrix, preferred_element_type=jnp.float32
    )
    amino_number = lax.all_to_all(
        alignment_intermediate, "dap", split_axis=1, concat_axis=0, tiled=True
    )
    alignment_target_tensor = vertical_softmax_mixing(
        amino_number, vertical_scale_factor, vertical_projection_matrix, vertical_final_matrix
    )
    alignment_depth = alignment_target_tensor.shape[0]
    alignments_each_slice = alignment_depth // rep_count
    first_alignment_entry = rep_index * alignments_each_slice
    chosen_alignments = lax.dynamic_slice_in_dim(
        alignment_target_tensor, first_alignment_entry, alignments_each_slice, 0
    )
    tensorial_standardized = standardize_features(chosen_alignments, tensorial_scale_factor).astype(
        jnp.bfloat16
    )
    tensorial_result = jnp.dot(
        tensorial_standardized, tensorial_factor_matrix, preferred_element_type=jnp.float32
    ).astype(jnp.bfloat16)
    operand = tensorial_factor_matrix.shape[1] // 2
    left_side = tensorial_result[..., :operand]
    local_res = left_side.shape[1]
    right_flat = tensorial_result[..., operand:].reshape(alignments_each_slice, local_res * operand)
    right_all = lax.all_gather(right_flat, "dap", axis=1, tiled=True).reshape(
        alignments_each_slice, chain_extent, operand
    )
    outer_prod = jnp.einsum(
        "sic,sje->jice", left_side, right_all, preferred_element_type=jnp.float32
    ) * (1.0 / alignment_depth)
    flattened = outer_prod.astype(jnp.bfloat16).reshape(chain_extent, local_res, operand * operand)
    partial_sum = jnp.dot(flattened, tensorial_final_matrix, preferred_element_type=jnp.float32)
    summed = lax.psum_scatter(partial_sum, "rep", scatter_dimension=0, tiled=True)
    couple_target_tensor = couple_source_tensor + jnp.swapaxes(summed, 0, 1)
    return (alignment_target_tensor, couple_target_tensor)


def solution(mesh):
    return jax.shard_map(
        shards,
        mesh=mesh,
        in_specs=(
            P("dap", None, None),
            P("dap", "rep", None),
            P(),
            P(),
            P(),
            P(),
            P(),
            P(),
            P(),
            P(),
            P(),
            P(),
            P(),
        ),
        out_specs=(P(None, "dap", None), P("dap", "rep", None)),
        check_vma=False,
    )
```

profile of v0, /device:TPU:1, one launch (start us, length us, event | category | flops | bytes accessed | tf_op | source)
XLA Modules:
  0.0 519.2 jit_solution(2330058972247540209)
XLA Ops:
  7.2 0.0 all-gather.4.cloned.1.call-start
  7.2 1.1 reduce_sum.92
  8.4 1.2 multiply_reduce_fusion.4
  9.6 1.9 fusion.22
  11.5 0.0 all-gather.4.cloned.1.call-update
  11.5 0.0 all-gather.6.cloned.1.call-start
  11.6 126.8 %all-gather.4.cloned.1.call-done = bf16[8,512,128]{2,0,1:T(8,128)(2,1)} async-done(((bf16[8,4,128]{2,0,1:T(8,128)(2,1)}), bf16[8,512,128]{2,0,1:T(8,128)(2,1)}) %all-gather.4.cloned.1.call-update) | async-done | bytes 1048592 | tf_op jit(solution)/shard_map/all_gather | solution.py:98
  138.4 0.0 all-gather.6.cloned.1.call-update
  138.4 1.4 reduce_sum.90
  139.9 1.6 multiply_reduce_fusion.2
  141.5 3.4 convolution_convert_fusion.1
  144.9 77.3 %all-gather.6.cloned.1.call-done = bf16[8,512,512]{2,0,1:T(8,128)(2,1)} async-done(((bf16[8,512,128]{2,0,1:T(8,128)(2,1)}), bf16[8,512,512]{2,0,1:T(8,128)(2,1)}) %all-gather.6.cloned.1.call-update) | async-done | bytes 4194320 | tf_op jit(solution)/shard_map/all_gather | solution.py:102
  222.2 7.6 %copy.63 = bf16[8,512,512]{1,2,0:T(8,128)(2,1)} copy(bf16[8,512,512]{2,0,1:T(8,128)(2,1)} %all-gather.6.cloned.1.call-done) | data formatting | bytes 8388608 | tf_op jit(solution)/shard_map/while | solution.py:116
  229.8 24.6 %while.10 = (s32[]{:T(128)}, bf16[2,512,256]{1,2,0:T(8,128)(2,1)S(1)}, bf16[2,512,1024]{2,1,0:T(8,128)(2,1)}, bf16[8,512,512]{1,2,0:T(8,128)(2,1)}, s32[]{:T(128)}) while((s32[]{:T(128)}, bf16[2,512,256]{1,2,0:T(8,128)(2,1)S(1)}, bf16[2,512,1024]{2,1,0:T(8,128)(2,1)}, bf16[8,512,512]{1,2,0:T(8,128)(2,1)}, s32[]{:T(128)}) %tuple.35), condition=%wide.region_7.8_spmd, body=%wide.region_4.7_spmd.sunk | while | flops 426513408 | bytes 17072204 | solution.py:116
  229.8 1.3 constant_dynamic-slice_fusion.2
  231.2 0.5 copy.107
  231.7 0.1 fusion.80
  231.8 4.6 fusion.81
  236.3 5.6 %fusion.82 = f32[8,32,512]{2,1,0:T(8,128)S(1)} fusion(bf16[512,8,32]{0,2,1:T(8,128)(2,1)S(1)} %bitcast.107, f32[8,512]{1,0:T(8,128)S(1)} %fusion.81, bf16[8,512,512]{1,2,0:T(8,128)(2,1)} %get-tuple-element.101, bf16[512,8,32]{0,2,1:T(8,128)(2,1)S(1)} %bitcast.106, bf16[512,8,32]{0,2,1:T(8,128)(2,1)S(1)} %bitcast.104), kind=kOutput, calls=%fused_computation.6.clone.1 | convolution fusion | flops 281022976 | bytes 5521408 | tf_op jit(solution)/shard_map/while/body/eval_jaxpr/hqk,khd->qhd/dot_general | solution.py:30
  242.0 0.2 bitcast_dynamic-update-slice_fusion.2
  242.1 1.3 constant_dynamic-slice_fusion.2
  243.4 0.5 copy.107
  244.0 0.1 fusion.80
  244.1 4.6 fusion.81
  248.6 5.6 %fusion.82 = f32[8,32,512]{2,1,0:T(8,128)S(1)} fusion(bf16[512,8,32]{0,2,1:T(8,128)(2,1)S(1)} %bitcast.107, f32[8,512]{1,0:T(8,128)S(1)} %fusion.81, bf16[8,512,512]{1,2,0:T(8,128)(2,1)} %get-tuple-element.101, bf16[512,8,32]{0,2,1:T(8,128)(2,1)S(1)} %bitcast.106, bf16[512,8,32]{0,2,1:T(8,128)(2,1)S(1)} %bitcast.104), kind=kOutput, calls=%fused_computation.6.clone.1 | convolution fusion | flops 281022976 | bytes 5521408 | tf_op jit(solution)/shard_map/while/body/eval_jaxpr/hqk,khd->qhd/dot_general | solution.py:30
  254.2 0.2 bitcast_dynamic-update-slice_fusion.2
  254.4 0.8 copy-done.6
  255.2 1.8 convolution_add_fusion.1
  257.0 1.8 copy.65
  258.8 13.7 %all-to-all-start = ((f32[2,512,256]{2,0,1:T(2,128)}), f32[2,512,256]{2,0,1:T(2,128)S(1)}, u32[]{:S(2)}, u32[]{:S(2)}) async-start(f32[2,512,256]{2,0,1:T(2,128)} %copy.65), calls=%async_computation | async-start | bytes 2097152 | tf_op jit(solution)/shard_map/all_to_all | solution.py:120
  272.5 0.2 all-gather.8.cloned.1.call-start
  272.7 32.1 %all-to-all-done = f32[2,512,256]{2,0,1:T(2,128)S(1)} async-done(((f32[2,512,256]{2,0,1:T(2,128)}), f32[2,512,256]{2,0,1:T(2,128)S(1)}, u32[]{:S(2)}, u32[]{:S(2)}) %all-to-all-start) | async-done | bytes 1048608 | tf_op jit(solution)/shard_map/all_to_all | solution.py:120
  304.8 0.3 copy.105
  305.0 0.3 fusion.50
  305.4 0.6 multiply_reduce_fusion.1
  306.1 0.1 copy.69
  306.2 0.8 copy.67
  307.0 1.7 all_to_all.16
  308.7 0.1 copy.73
  308.8 0.1 copy.74
  308.9 0.1 copy.70
  309.0 2.0 convolution_convert_fusion
  311.0 1.1 fusion.53
  312.1 2.1 copy.75
  314.2 2.1 copy.76
  316.3 1.0 copy.77
  317.3 7.4 %fusion.54 = (f32[4,8,256]{2,1,0:T(8,128)S(1)}, f32[4,8,256,256]{2,3,1,0:T(8,128)}) fusion(bf16[256,4,8,32]{0,3,2,1:T(8,128)(2,1)} %bitcast.112, bf16[256,4,8,32]{0,3,2,1:T(8,128)(2,1)} %bitcast.113), kind=kOutput, calls=%fused_computation.84 | convolution fusion | flops 140509440 | bytes 9469952 | tf_op jit(solution)/shard_map/sub | solution.py:52
  324.7 5.3 %fusion.19 = f32[4,8,32,256]{3,2,1,0:T(8,128)} fusion(bf16[256,4,8,32]{0,3,2,1:T(8,128)(2,1)S(1)} %bitcast.111, f32[4,8,256,256]{2,3,1,0:T(8,128)} %get-tuple-element.56, f32[4,8,256]{2,1,0:T(8,128)S(1)} %get-tuple-element.55), kind=kOutput, calls=%fused_computation.25 | convolution fusion | flops 138412032 | bytes 9994240 | tf_op jit(solution)/shard_map/bhst,tbhd->sbhd/dot_general | solution.py:54
  330.1 2.5 copy.79
  332.6 2.0 convolution_add_fusion
  334.6 0.1 dynamic-slice_reduce_fusion
  334.7 0.2 multiply_reduce_fusion.3
  334.9 0.6 copy-done.2
  335.6 0.3 convolution_convert_fusion.2
  335.8 0.6 slice.44
  336.5 0.0 all-gather.8.cloned.1.call-update
  336.5 0.3 reduce-scatter.2.cloned.1.call-start
  336.7 133.9 %all-gather.8.cloned.1.call-done = bf16[64,16384]{0,1:T(8,128)(2,1)} async-done(((bf16[64,128]{0,1:T(8,128)(2,1)}), bf16[64,16384]{0,1:T(8,128)(2,1)}) %all-gather.8.cloned.1.call-update) | async-done | bytes 2097168 | tf_op jit(solution)/shard_map/all_gather | solution.py:142
  470.7 7.1 %fusion.15 = bf16[512,4,32,32]{0,2,1,3:T(8,128)(2,1)S(1)} fusion(bf16[64,512,32,1]{0,2,1,3:T(8,128)(2,1)} %bitcast.108, bf16[64,4,64]{0,2,1:T(8,128)(2,1)S(1)} %convolution_convert_fusion.2), kind=kOutput, calls=%fused_computation.21 | convolution fusion | flops 272629760 | bytes 6324224 | tf_op jit(solution)/shard_map/sic,sje->jice/dot_general | solution.py:145
  477.8 2.4 copy.81
  480.2 2.3 fusion.35
  482.6 1.6 copy.83
  484.2 26.8 %reduce-scatter.2.cloned.1.call-done = f32[128,4,128]{2,0,1:T(8,128)} async-done(((f32[512,4,128]{2,0,1:T(8,128)}), f32[128,4,128]{2,0,1:T(8,128)}) %reduce-scatter.2.cloned.1.call-update) | async-done | bytes 262160 | tf_op jit(solution)/shard_map/reduce_scatter | solution.py:150
  511.0 1.7 bitcast_add_fusion
  (34 shorter events, 0.2 us)
Async XLA Ops:
  7.2 134.3 %copy-start = (bf16[256,1024]{1,0:T(8,128)(2,1)S(1)}, bf16[256,1024]{1,0:T(8,128)(2,1)}, u32[]{:S(2)}) copy-start(bf16[256,1024]{1,0:T(8,128)(2,1)} %param.18) | copy-start | bytes 1572868
  7.2 131.2 %all-gather.4.cloned.1.call-start = ((), (), s32[]{:S(2)}) async-start(), calls=%async_computation.2 | async-start | bytes 1056768 | tf_op jit(solution)/shard_map/all_gather | solution.py:98
  11.5 210.7 %all-gather.6.cloned.1.call-start = ((), (), s32[]{:S(2)}) async-start(), calls=%async_computation.3 | async-start | bytes 5242880 | tf_op jit(solution)/shard_map/all_gather | solution.py:102
  229.8 25.4 %copy-start.8 = (bf16[256,256]{1,0:T(8,128)(2,1)S(1)}, bf16[256,256]{1,0:T(8,128)(2,1)}, u32[]{:S(2)}) copy-start(bf16[256,256]{1,0:T(8,128)(2,1)} %param.21) | copy-start | bytes 393220
  254.4 0.8 copy-start.6
  255.2 53.8 %copy-start.5 = (bf16[256,1024]{1,0:T(8,128)(2,1)S(1)}, bf16[256,1024]{1,0:T(8,128)(2,1)}, u32[]{:S(2)}) copy-start(bf16[256,1024]{1,0:T(8,128)(2,1)} %param.23) | copy-start | bytes 1572868
  255.2 53.8 %copy-start.9 = (f32[256]{0:T(256)S(1)}, f32[256]{0:T(256)}, u32[]{:S(2)}) copy-start(f32[256]{0:T(256)} %param.22) | copy-start | bytes 3076
  258.8 46.0 %all-to-all-start = ((f32[2,512,256]{2,0,1:T(2,128)}), f32[2,512,256]{2,0,1:T(2,128)S(1)}, u32[]{:S(2)}, u32[]{:S(2)}) async-start(f32[2,512,256]{2,0,1:T(2,128)} %copy.65), calls=%async_computation | async-start | bytes 2097152 | tf_op jit(solution)/shard_map/all_to_all | solution.py:120
  272.5 198.2 %all-gather.8.cloned.1.call-start = ((), (), s32[]{:S(2)}) async-start(), calls=%async_computation.4 | async-start | bytes 4227072 | tf_op jit(solution)/shard_map/all_gather | solution.py:142
  317.3 7.4 %copy-start.4 = (bf16[256,4,256]{0,2,1:T(8,128)(2,1)S(1)}, bf16[256,4,256]{0,2,1:T(8,128)(2,1)}, u32[]{:S(2)}) copy-start(bf16[256,4,256]{0,2,1:T(8,128)(2,1)} %copy.75) | copy-start | bytes 1572868
  324.7 7.9 %copy-start.10 = (bf16[256,256]{1,0:T(8,128)(2,1)S(1)}, bf16[256,256]{1,0:T(8,128)(2,1)}, u32[]{:S(2)}) copy-start(bf16[256,256]{1,0:T(8,128)(2,1)} %param.24) | copy-start | bytes 393220
  324.7 10.8 %copy-start.11 = (bf16[256,64]{0,1:T(8,128)(2,1)S(1)}, bf16[256,64]{0,1:T(8,128)(2,1)}, u32[]{:S(2)}) copy-start(bf16[256,64]{0,1:T(8,128)(2,1)} %param.26) | copy-start | bytes 98308
  324.7 10.8 %copy-start.12 = (f32[256]{0:T(256)S(1)}, f32[256]{0:T(256)}, u32[]{:S(2)}) copy-start(f32[256]{0:T(256)} %param.25) | copy-start | bytes 3076
  334.6 1.0 copy-start.2
  336.5 174.5 %reduce-scatter.2.cloned.1.call-start = ((), (), s32[]{:S(2)}) async-start(), calls=%async_computation.5 | async-start | bytes 1310720 | tf_op jit(solution)/shard_map/reduce_scatter | solution.py:150
  470.7 9.6 %copy-start.7 = (bf16[1024,128]{1,0:T(8,128)(2,1)S(1)}, bf16[1024,128]{1,0:T(8,128)(2,1)}, u32[]{:S(2)}) copy-start(bf16[1024,128]{1,0:T(8,128)(2,1)} %param.27) | copy-start | bytes 786436
  477.8 4.8 copy-start.3
  477.8 33.2 %copy-start.1 = (f32[4,128,128]{2,1,0:T(8,128)S(1)}, f32[4,128,128]{2,1,0:T(8,128)}, u32[]{:S(2)}) copy-start(f32[4,128,128]{2,1,0:T(8,128)} %param.16) | copy-start | bytes 786436
Sparse Core Ops, SparseCore 0:
  13.0 125.3 all-gather.3
  140.5 81.6 all-gather.5
  336.6 134.0 all-gather.7
  482.7 28.2 reduce-scatter.1
where the time goes:
time: 520 us; the launch traced here: 519 us
  waiting for transfers between devices  397 us (76%)
  matrix products  53.7 us (10%)
  local copies, waits for them, and re-layouts  31.4 us (6%)
  starting transfers between devices  14.2 us (3%)
  between operations  14 us (3%)
  other arithmetic  8.74 us (2%)
    all_gather x1, waiting for transfers between devices, shards(): lax.all_gather(right_flat, 'dap', axis=1, tiled=True)  134 us
    all_gather x1, waiting for transfers between devices, shards(): rows_bias = lax.all_gather(local_bias, 'dap', axis=1, tiled=True)  127 us
    all_gather x1, waiting for transfers between devices, shards(): full_bias = lax.all_gather(rows_bias, 'rep', axis=2, tiled=True)  77.3 us
    all_to_all x1, waiting for transfers between devices, shards(): lax.all_to_all(alignment_intermediate, 'dap', split_axis=1, concat_axis=0...  32.1 us
    reduce_scatter x1, waiting for transfers between devices, shards(): lax.psum_scatter(partial_sum, 'rep', scatter_dimension=0, tiled=True)  26.8 us
    all_to_all x1, starting transfers between devices, shards(): lax.all_to_all(alignment_intermediate, 'dap', split_axis=1, concat_axis=0...  13.7 us
    dot_general x2, matrix products, attend(): jnp.einsum('hqk,khd->qhd', weights, value_heads, preferred_element_type=j...  11.2 us
  transfers between devices with their start and end apart: 5, of which 5 were waited for; matrix products, arithmetic and copies ran while one was open for 2% of the time, Pallas kernels for 0%

commit v1 on v0

v1 whole, which is shorter than its diff:
```python
import math

import jax
import jax.numpy as jnp
from jax import lax
from jax.experimental import pallas as pl
from jax.experimental.pallas import tpu as pltpu
from jax.sharding import PartitionSpec as P

HEADS = 8
HEAD_DIM = 32
FEAT = HEADS * HEAD_DIM
CZ = 128
ROWS = 256
RES = 512
FACTOR = 32
LOG2E = math.log2(math.e)
LOGIT_SCALE = HEAD_DIM ** (-0.5) * LOG2E
MESH = pl.DeviceIdType.MESH
F32 = jnp.float32
BF16 = jnp.bfloat16

BIAS1, BIAS_Y, BIAS_X, BIAS_C, MSA1, MSA2, LEFT, FINAL, RIGHT1, RIGHT_Y, RIGHT_X, RIGHT_C = range(12)
PHASES = 12


def layer_norm(values, gain):
    average = jnp.mean(values, axis=-1, keepdims=True)
    centred = values - average
    variance = jnp.mean(centred * centred, axis=-1, keepdims=True)
    return (centred * lax.rsqrt(variance + 1e-05) * gain).astype(BF16)


def dot(a, b):
    return lax.dot_general(a, b, (((1,), (0,)), ((), ())), preferred_element_type=F32)


def dot_nt(a, b):
    return lax.dot_general(a, b, (((1,), (1,)), ((), ())), preferred_element_type=F32)


def head_mask():
    head = lax.broadcasted_iota(jnp.int32, (HEADS, FEAT), 0)
    channel = lax.broadcasted_iota(jnp.int32, (HEADS, FEAT), 1) // HEAD_DIM
    return (head == channel).astype(F32)


def expand_heads(queries):
    n = queries.shape[0]
    spread = jnp.broadcast_to(queries[:, None, :], (n, HEADS, FEAT))
    return (spread * head_mask()[None]).reshape(n * HEADS, FEAT).astype(BF16)


def merge_heads(attended, inverse):
    n = attended.shape[0] // HEADS
    scaled = (attended * inverse).reshape(n, HEADS, FEAT) * head_mask()[None]
    return jnp.sum(scaled, axis=1)


def kernel(
    msa, pair, g_row, w_row, g_pair, w_bias, wo_row, g_col, w_col, wo_col, g_opm, w_fac, w_fin,
    out_msa, out_pair,
    bias_src, bias_in, bias, queries, gates, keys, values, logits, weights, denom, staged, msa_src, msa_in,
    unpacked, col_src, col_in, col_logits, col_weights, col_denom, natural, final, left_src, left, right_src, right,
    right_f, final_f, final_w, outer, update, msa_halves, spread,
    send, recv,
):
    dap = lax.axis_index("dap")
    rep = lax.axis_index("rep")
    x = dap // 32
    y = (dap // 4) % 8
    xy = dap // 4
    zc = dap % 4
    zh = zc // 2
    core = zc % 2
    member = core * 2 + zh

    def device(xy_, zh_, core_):
        return xy_ * 4 + zh_ * 2 + core_

    barrier = pltpu.get_barrier_semaphore()

    def greet(dap_, rep_):
        pl.semaphore_signal(barrier, inc=1, device_id=(dap_, rep_), device_id_type=MESH)

    def greet_xy(step, _):
        greet(device((xy + step) % 32, zh, core), rep)
        return 0

    lax.fori_loop(1, 32, greet_xy, 0)
    for step in range(1, 8):
        other = (zh * 4 + rep + step) % 8
        greet(device(xy, other // 4, core), other % 4)
    greet(device(xy, zh, 1 - core), rep)
    greet(device(xy, 1 - zh, 1 - core), rep)
    mirror = rep * 8 + y
    greet(device(mirror, 1 - zh, core), x)

    @pl.when(x != rep)
    def _():
        greet(device(mirror, zh, core), x)

    def push(src, dst, phase, dap_, rep_):
        pltpu.make_async_remote_copy(
            src_ref=src, dst_ref=dst, send_sem=send.at[phase], recv_sem=recv.at[phase],
            device_id=(dap_, rep_), device_id_type=MESH,
        ).start()

    def arrived(shaped, phase):
        pltpu.make_async_copy(shaped, shaped, recv.at[phase]).wait()

    def drained(shaped, phase):
        pltpu.make_async_copy(shaped, shaped, send.at[phase]).wait()

    def push_y(buffer, phase):
        for step in range(1, 8):
            block = buffer.at[x, y, core]
            push(block, block, phase, device(x * 8 + (y + step) % 8, zh, core), rep)

    def push_x(buffer, phase):
        for step in range(1, 4):
            block = buffer.at[x, :, core]
            push(block, block, phase, device(((x + step) % 4) * 8 + y, zh, core), rep)

    def push_c(buffer, phase):
        block = buffer.at[:, :, core]
        push(block, block, phase, device(xy, zh, 1 - core), rep)

    ln_pair = layer_norm(pair[...].reshape(4 * 128, CZ), g_pair[...])
    head_bias = dot_nt(w_bias[...], ln_pair) * LOG2E
    for a in range(4):
        bias_src[a] = head_bias[:, a * 128 : (a + 1) * 128]

    pl.semaphore_wait(barrier, 41 + jnp.where(x != rep, 1, 0))

    for step in range(1, 8):
        other = (zh * 4 + rep + step) % 8
        push(bias_src.at[other % 4], bias_in.at[zh * 4 + rep], BIAS1, device(xy, other // 4, core), other % 4)
    bias_in[zh * 4 + rep] = bias_src[rep]

    for s in range(2):
        tokens = layer_norm(msa[s], g_row[...])
        projected = dot(tokens, w_row[:, FEAT : 3 * FEAT]).astype(BF16)
        keys[s] = projected[:, :FEAT]
        values[s] = projected[:, FEAT:]
        for half in range(2):
            msa_halves[s, half] = msa[s, :, half * 128 : (half + 1) * 128]
            for h_ in range(2):
                for c_ in range(2):
                    queries[s, half, pl.ds(c_ * 2 + h_, 32, stride=4), :] = msa_halves[
                        s, half, pl.ds(8 * h_ + 4 * c_ + rep, 32, stride=16), :
                    ]

    arrived(bias_in.at[pl.ds(0, 7)], BIAS1)
    block = jnp.concatenate(
        [jnp.concatenate([bias_in[h_ * 4 + r_] for r_ in range(4)], axis=1) for h_ in range(2)], axis=0
    )
    bias[x, y, core] = block.astype(BF16)
    push_y(bias, BIAS_Y)

    def row_logits(s):
        tokens = layer_norm(jnp.concatenate([queries[s, 0], queries[s, 1]], axis=1), g_row[...])
        wide = dot(tokens, w_row[:, :FEAT]) * LOGIT_SCALE
        gates[s] = jax.nn.sigmoid(dot(tokens, w_row[:, 3 * FEAT :]))
        logits[s] = dot_nt(expand_heads(wide), keys[s]).reshape(32, 2, 16, RES)

    row_logits(0)
    arrived(bias.at[0, pl.ds(0, 7), 0], BIAS_Y)
    push_x(bias, BIAS_X)
    row_logits(1)
    final_f[...] = w_fin[...].astype(F32)
    for e in range(FACTOR):
        final_w[pl.ds(e * FACTOR, FACTOR), :] = final_f[pl.ds(e, FACTOR, stride=FACTOR), :].astype(BF16)
    arrived(bias.at[pl.ds(0, 3), :, 0], BIAS_X)
    push_c(bias, BIAS_C)

    def row_softmax(group, which):
        rows = pl.ds(group * 4, 4)
        offset = bias[group // 2, pl.ds((group % 2) * 4, 4), which].astype(F32).reshape(64, RES)
        for s in range(2):
            raw = logits[s, rows, which].reshape(64, RES) + offset
            top = jnp.max(raw, axis=-1, keepdims=True)
            powers = jnp.exp2(raw - top)
            total = jnp.sum(powers, axis=-1, keepdims=True)
            weights[s, rows, which] = powers.astype(BF16).reshape(4, 16, RES)
            denom[s, rows, which] = jnp.broadcast_to(1.0 / total, (64, 128)).reshape(4, 16, 128)
        return which

    lax.fori_loop(0, 8, row_softmax, core)
    arrived(bias.at[:, :, 0], BIAS_C)
    lax.fori_loop(0, 8, row_softmax, 1 - core)
    for s in range(2):
        attended = dot(weights[s].reshape(1024, RES), values[s])
        merged = merge_heads(attended, denom[s].reshape(1024, 128)[:, :1])
        gated = (merged * gates[s]).astype(BF16)
        change = dot(gated, wo_row[...])
        for half in range(2):
            staged[pl.ds(s * 2 + half, 128, stride=4), :] = queries[s, half] + change[:, half * 128 : (half + 1) * 128]
    msa_src[...] = staged[...].astype(BF16).reshape(32, 16, 128)

    def push_msa(step, _):
        other = (xy + step) % 32
        push(msa_src.at[other], msa_in.at[xy], MSA1, device(other, zh, core), rep)
        return 0

    lax.fori_loop(1, 32, push_msa, 0)
    msa_in[xy] = msa_src[xy]
    arrived(msa_in.at[pl.ds(0, 31)], MSA1)
    unpacked[...] = msa_in[...].astype(F32).reshape(512, 128)
    for target in range(4):
        parts = [
            jnp.concatenate(
                [unpacked[pl.ds(target * 4 + s * 2 + half, 32, stride=16), :] for half in range(2)], axis=1
            )
            for s in range(2)
        ]
        col_src[target] = jnp.concatenate(parts, axis=0).astype(BF16)
    for step in range(1, 4):
        other = (member + step) % 4
        push(col_src.at[other], col_in.at[member], MSA2, device(xy, other % 2, other // 2), rep)
    col_in[member] = col_src[member]
    arrived(col_in.at[pl.ds(0, 3)], MSA2)

    middle = col_in[...].astype(F32).reshape(ROWS, FEAT)
    tokens = layer_norm(middle, g_col[...])
    projected = dot(tokens, w_col[...])
    wide = expand_heads(projected[:, :FEAT] * LOGIT_SCALE)
    col_keys = projected[:, FEAT : 2 * FEAT].astype(BF16)
    col_values = projected[:, 2 * FEAT : 3 * FEAT].astype(BF16)
    col_gates = jax.nn.sigmoid(projected[:, 3 * FEAT :])
    col_logits[...] = dot_nt(wide, col_keys)

    def col_softmax(group, _):
        rows = pl.ds(pl.multiple_of(group * 128, 128), 128)
        raw = col_logits[rows, :]
        top = jnp.max(raw, axis=-1, keepdims=True)
        powers = jnp.exp2(raw - top)
        total = jnp.sum(powers, axis=-1, keepdims=True)
        col_weights[rows, :] = powers.astype(BF16)
        col_denom[rows, :] = jnp.broadcast_to(1.0 / total, (128, 128))
        return 0

    lax.fori_loop(0, 16, col_softmax, 0)
    attended = dot(col_weights[...], col_values)
    merged = merge_heads(attended, col_denom[...][:, :1])
    gated = (merged * col_gates).astype(BF16)
    target_rows = middle + dot(gated, wo_col[...])

    ln_opm = layer_norm(target_rows, g_opm[...])
    factors = dot_nt(w_fac[...], ln_opm)
    right_src[...] = factors[FACTOR:].astype(BF16)
    left_src[...] = (factors[:FACTOR] * (1.0 / ROWS)).astype(BF16)
    push(right_src, right.at[rep, y, core, zh], RIGHT1, device(mirror, 1 - zh, core), x)

    @pl.when(x != rep)
    def _():
        push(right_src, right.at[rep, y, core, zh], RIGHT1, device(mirror, zh, core), x)

    @pl.when(x == rep)
    def _():
        right[rep, y, core, zh] = right_src[...]

    for step in range(1, 4):
        push(left_src, left.at[rep], LEFT, dap, (rep + step) % 4)
    left[rep] = left_src[...]
    for m_ in range(4):
        for s in range(2):
            start = (m_ * 2 + s) * 32
            for half in range(2):
                natural[half, pl.ds((m_ % 2) * 4 + (m_ // 2) * 2 + s, 32, stride=8), :] = target_rows[
                    start : start + 32, half * 128 : (half + 1) * 128
                ]
    final[rep] = jnp.concatenate([natural[0], natural[1]], axis=1).astype(BF16)
    for step in range(1, 4):
        push(final.at[rep], final.at[rep], FINAL, dap, (rep + step) % 4)

    @pl.when(x != rep)
    def _():
        arrived(right.at[0, 0, 0], RIGHT1)

    @pl.when(x == rep)
    def _():
        arrived(right_src, RIGHT1)

    push_y(right, RIGHT_Y)
    arrived(right.at[0, pl.ds(0, 7), 0], RIGHT_Y)
    push_x(right, RIGHT_X)
    arrived(right.at[pl.ds(0, 3), :, 0], RIGHT_X)
    push_c(right, RIGHT_C)
    arrived(left.at[pl.ds(0, 3)], LEFT)
    left_all = left[...].reshape(4 * FACTOR, ROWS)
    arrived(right.at[:, :, 0], RIGHT_C)

    for half in range(2):
        right_f[half] = right[..., half * 128 : (half + 1) * 128].astype(F32).reshape(128 * FACTOR, 128)
    for e in range(FACTOR):
        operand = jnp.concatenate(
            [right_f[half, pl.ds(e, 128, stride=FACTOR), :] for half in range(2)], axis=1
        ).astype(BF16)
        product = dot_nt(left_all, operand).astype(BF16)
        for i in range(4):
            outer[pl.ds(e * FACTOR, FACTOR), i * 128 : (i + 1) * 128] = product[i * FACTOR : (i + 1) * FACTOR]
    flat = lax.dot_general(final_w[...], outer[...], (((0,), (0,)), ((), ())), preferred_element_type=F32)
    for i in range(4):
        update[i] = flat[:, i * 128 : (i + 1) * 128].T
        for x_ in range(4):
            for m_ in range(4):
                here = pl.ds(8 * (m_ % 2) + 4 * (m_ // 2) + x_, 8, stride=16)
                out_pair[i, here, :] = pair[i, here, :] + update[i, pl.ds(x_ * 32 + m_, 8, stride=4), :]

    arrived(final.at[pl.ds(0, 3)], FINAL)
    for half in range(2):
        for r_ in range(4):
            spread[half, pl.ds(r_, ROWS, stride=4), :] = final[r_, :, half * 128 : (half + 1) * 128].astype(F32)
        out_msa[:, half * 128 : (half + 1) * 128] = spread[half]

    drained(bias_in.at[pl.ds(0, 7)], BIAS1)
    drained(bias.at[0, pl.ds(0, 7), 0], BIAS_Y)
    drained(bias.at[pl.ds(0, 3), :, 0], BIAS_X)
    drained(bias.at[:, :, 0], BIAS_C)
    drained(msa_in.at[pl.ds(0, 31)], MSA1)
    drained(col_in.at[pl.ds(0, 3)], MSA2)
    drained(left.at[pl.ds(0, 3)], LEFT)
    drained(final.at[pl.ds(0, 3)], FINAL)

    @pl.when(x != rep)
    def _():
        drained(right.at[0, 0, 0], RIGHT1)

    @pl.when(x == rep)
    def _():
        drained(right_src, RIGHT1)

    drained(right.at[0, pl.ds(0, 7), 0], RIGHT_Y)
    drained(right.at[pl.ds(0, 3), :, 0], RIGHT_X)
    drained(right.at[:, :, 0], RIGHT_C)


def shards(
    alignment_source_tensor,
    couple_source_tensor,
    horizontal_scale_factor,
    horizontal_projection_matrix,
    couple_scale_factor,
    couple_offset_matrix,
    horizontal_final_matrix,
    vertical_scale_factor,
    vertical_projection_matrix,
    vertical_final_matrix,
    tensorial_scale_factor,
    tensorial_factor_matrix,
    tensorial_final_matrix,
):
    vmem = pl.BlockSpec(memory_space=pltpu.VMEM)
    scratch = [
        pltpu.VMEM((4, 8, 128), F32),
        pltpu.VMEM((8, 8, 128), F32),
        pltpu.VMEM((4, 8, 2, 16, RES), BF16),
        pltpu.VMEM((2, 2, 128, 128), F32),
        pltpu.VMEM((2, 128, FEAT), F32),
        pltpu.VMEM((2, RES, FEAT), BF16),
        pltpu.VMEM((2, RES, FEAT), BF16),
        pltpu.VMEM((2, 32, 2, 16, RES), F32),
        pltpu.VMEM((2, 32, 2, 16, RES), BF16),
        pltpu.VMEM((2, 32, 2, 16, 128), F32),
        pltpu.VMEM((512, 128), F32),
        pltpu.VMEM((32, 16, 128), BF16),
        pltpu.VMEM((32, 16, 128), BF16),
        pltpu.VMEM((512, 128), F32),
        pltpu.VMEM((4, 64, FEAT), BF16),
        pltpu.VMEM((4, 64, FEAT), BF16),
        pltpu.VMEM((ROWS * HEADS, ROWS), F32),
        pltpu.VMEM((ROWS * HEADS, ROWS), BF16),
        pltpu.VMEM((ROWS * HEADS, 128), F32),
        pltpu.VMEM((2, ROWS, 128), F32),
        pltpu.VMEM((4, ROWS, FEAT), BF16),
        pltpu.VMEM((FACTOR, ROWS), BF16),
        pltpu.VMEM((4, FACTOR, ROWS), BF16),
        pltpu.VMEM((FACTOR, ROWS), BF16),
        pltpu.VMEM((4, 8, 2, 2, FACTOR, ROWS), BF16),
        pltpu.VMEM((2, 128 * FACTOR, 128), F32),
        pltpu.VMEM((FACTOR * FACTOR, CZ), F32),
        pltpu.VMEM((FACTOR * FACTOR, CZ), BF16),
        pltpu.VMEM((FACTOR * FACTOR, 512), BF16),
        pltpu.VMEM((4, 128, CZ), F32),
        pltpu.VMEM((2, 2, RES, 128), F32),
        pltpu.VMEM((2, ROWS * 4, 128), F32),
        pltpu.SemaphoreType.DMA((PHASES,)),
        pltpu.SemaphoreType.DMA((PHASES,)),
    ]
    out_msa, out_pair = pl.pallas_call(
        kernel,
        out_shape=(
            jax.ShapeDtypeStruct((ROWS * 4, FEAT), F32),
            jax.ShapeDtypeStruct((4, 128, CZ), F32),
        ),
        in_specs=[vmem] * 13,
        out_specs=(vmem, vmem),
        scratch_shapes=scratch,
        compiler_params=pltpu.CompilerParams(
            collective_id=0, has_side_effects=True, vmem_limit_bytes=48 * 1024 * 1024
        ),
    )(
        alignment_source_tensor,
        couple_source_tensor,
        horizontal_scale_factor.reshape(1, FEAT),
        horizontal_projection_matrix,
        couple_scale_factor.reshape(1, CZ),
        couple_offset_matrix.T,
        horizontal_final_matrix,
        vertical_scale_factor.reshape(1, FEAT),
        vertical_projection_matrix,
        vertical_final_matrix,
        tensorial_scale_factor.reshape(1, FEAT),
        tensorial_factor_matrix.T,
        tensorial_final_matrix,
    )
    return out_msa.reshape(ROWS, 4, FEAT), out_pair


def solution(mesh):
    return jax.shard_map(
        shards,
        mesh=mesh,
        in_specs=(P("dap", None, None), P("dap", "rep", None)) + (P(),) * 11,
        out_specs=(P(None, "dap", None), P("dap", "rep", None)),
        check_vma=False,
    )
```

time: 520 us -> 99.9 us (0.19)
  waiting for transfers between devices: 397 us -> 0 us
  Pallas kernels: 0 us -> 88.3 us
  matrix products: 53.7 us -> 0 us
  local copies, waits for them, and re-layouts: 31.4 us -> 10.4 us
  starting transfers between devices: 14.2 us -> 0 us
  between operations: 14 us -> 0.69 us
  other arithmetic: 8.74 us -> 0 us
    all_gather x3 -> x0, waiting for transfers between devices: 338 us -> none  [the longest x1 134 us: shards(): lax.all_gather(right_flat, 'dap', axis=1, tiled=True)]
    pallas_call x0 -> x1, Pallas kernels: none -> 88.3 us  [shards(): pl.pallas_call(kernel, out_shape=(jax.ShapeDtypeStruct((ROWS * 4, FEAT),...]
    dot_general x11 -> x0, matrix products: 37.3 us -> none  [the longest x2 11.2 us: attend(): jnp.einsum('hqk,khd->qhd', weights, value_heads, preferred_element_type=j...]
    all_to_all x1 -> x0, waiting for transfers between devices: 32.1 us -> none  [shards(): lax.all_to_all(alignment_intermediate, 'dap', split_axis=1, concat_axis=0...]
    reduce_scatter x1 -> x0, waiting for transfers between devices: 26.8 us -> none  [shards(): lax.psum_scatter(partial_sum, 'rep', scatter_dimension=0, tiled=True)]
    sub x3 -> x0, matrix products: 16.5 us -> none  [the longest x2 9.11 us: attend(): exponent = jnp.exp(logits - maximum)]
    all_to_all x1 -> x0, starting transfers between devices: 13.7 us -> none  [shards(): lax.all_to_all(alignment_intermediate, 'dap', split_axis=1, concat_axis=0...]
    while x1 -> x0, local copies, waits for them, and re-layouts: 7.6 us -> none  [shards(): horizontal_sigmoid_masked = lax.map(row_whole, horizontal_result)]
  transfers between devices with their start and end apart: 5 -> 0, of which waited for: 5 -> 0; matrix products, arithmetic and copies ran while one was open for 2% -> 0% of each run, Pallas kernels for 0% -> 0%
where the time goes in v1:
time: 99.9 us; the launch traced here: 99.4 us
  Pallas kernels  88.3 us (88%)
  local copies, waits for them, and re-layouts  10.4 us (10%)
    pallas_call x1, Pallas kernels, shards(): pl.pallas_call(kernel, out_shape=(jax.ShapeDtypeStruct((ROWS * 4, FEAT),...  88.3 us
    unnamed x27, local copies, waits for them, and re-layouts  9.16 us

profile of v1, /device:TPU:1, one launch (start us, length us, event | category | flops | bytes accessed | tf_op | source)
XLA Modules:
  0.0 99.4 jit_solution(690714670631884886)
XLA Ops:
  0.6 0.0 copy-start.10
  0.6 0.0 copy-start.11
  0.7 0.0 copy-start.8
  0.7 0.0 copy-start.9
  0.7 0.0 copy-start.12
  0.7 0.6 copy-done.10
  1.3 0.0 copy-done.11
  1.3 0.0 copy-done.8
  1.3 0.0 copy-done.9
  1.4 0.0 copy-done.12
  1.4 0.0 copy-start
  1.4 1.2 %copy-done = f32[2,512,256]{2,1,0:T(8,128)S(1)} copy-done((f32[2,512,256]{2,1,0:T(8,128)S(1)}, f32[2,512,256]{2,1,0:T(8,128)}, u32[]{:S(2)}) %copy-start) | copy-done | bytes 1048600
  2.6 0.0 copy-start.1
  2.6 1.0 %copy-done.1 = bf16[256,1024]{1,0:T(8,128)(2,1)S(1)} copy-done((bf16[256,1024]{1,0:T(8,128)(2,1)S(1)}, bf16[256,1024]{1,0:T(8,128)(2,1)}, u32[]{:S(2)}) %copy-start.1) | copy-done | bytes 524312
  3.6 0.0 copy-start.2
  3.6 1.0 %copy-done.2 = bf16[256,1024]{1,0:T(8,128)(2,1)S(1)} copy-done((bf16[256,1024]{1,0:T(8,128)(2,1)S(1)}, bf16[256,1024]{1,0:T(8,128)(2,1)}, u32[]{:S(2)}) %copy-start.2) | copy-done | bytes 524312
  4.7 0.0 copy-start.3
  4.7 0.9 copy-done.3
  5.6 0.0 copy-start.4
  5.6 0.9 copy-done.4
  6.6 0.0 copy-start.5
  6.6 0.9 copy-done.5
  7.5 0.0 copy-start.6
  7.5 0.9 copy-done.6
  8.4 0.0 copy-start.7
  8.4 0.8 copy-done.7
  9.1 88.3 %shard_map.140 = (f32[1024,256]{1,0:T(8,128)S(1)}, f32[4,128,128]{2,1,0:T(8,128)S(1)}) custom-call(f32[2,512,256]{2,1,0:T(8,128)S(1)} %copy-done, f32[4,128,128]{2,1,0:T(8,128)S(1)} %copy-done.3, f32[1,256]{1,0:T(1,128)S(1)} %bitcast.8, bf16[256,1024]{1,0:T(8,128)(2,1)S(1)} %copy-done.1, f32[1,128]{1,0:T(1,128)S(1)} %bitcast.11, bf16[8,128]{1,0:T(8,128)(2,1)S(1)} %bitcast.7, ...), custom_call_target="tpu_custom_call" | custom-call | tf_op jit(solution)/shard_map/pallas_call | solution.py:391
  97.4 1.3 %reshape.23 = f32[256,4,256]{2,1,0:T(4,128)} reshape(f32[1024,256]{1,0:T(8,128)S(1)} %get-tuple-element.4) | data formatting | bytes 2097152 | tf_op jit(solution)/shard_map/reshape | solution.py:418
  98.7 0.7 copy.16
Async XLA Ops:
  0.6 0.7 copy-start.10
  0.6 0.7 copy-start.11
  0.7 0.7 copy-start.8
  0.7 0.7 copy-start.9
  0.7 0.7 copy-start.12
  1.4 1.2 %copy-start = (f32[2,512,256]{2,1,0:T(8,128)S(1)}, f32[2,512,256]{2,1,0:T(8,128)}, u32[]{:S(2)}) copy-start(f32[2,512,256]{2,1,0:T(8,128)} %msa.1) | copy-start | bytes 3145732
  2.6 1.0 %copy-start.1 = (bf16[256,1024]{1,0:T(8,128)(2,1)S(1)}, bf16[256,1024]{1,0:T(8,128)(2,1)}, u32[]{:S(2)}) copy-start(bf16[256,1024]{1,0:T(8,128)(2,1)} %w_row.1) | copy-start | bytes 1572868
  3.6 1.0 %copy-start.2 = (bf16[256,1024]{1,0:T(8,128)(2,1)S(1)}, bf16[256,1024]{1,0:T(8,128)(2,1)}, u32[]{:S(2)}) copy-start(bf16[256,1024]{1,0:T(8,128)(2,1)} %w_col.1) | copy-start | bytes 1572868
  4.7 0.9 copy-start.3
  5.6 0.9 copy-start.4
  6.6 0.9 copy-start.5
  7.5 0.9 copy-start.6
  8.4 0.8 copy-start.7

commit v2 on v1

--- a/solution.py
+++ b/solution.py
@@ -20,8 +20,8 @@
 F32 = jnp.float32
 BF16 = jnp.bfloat16
 
-BIAS1, BIAS_Y, BIAS_X, BIAS_C, MSA1, MSA2, LEFT, FINAL, RIGHT1, RIGHT_Y, RIGHT_X, RIGHT_C = range(12)
-PHASES = 12
+BIAS1, BIAS_Y, BIAS_X, BIAS_C, MSA1, MSA2, LEFT, LEFT_X, LEFT_C, FINAL, RIGHT1, RIGHT_Y, RESULT = range(13)
+PHASES = 13
 
 
 def layer_norm(values, gain):
@@ -57,14 +57,23 @@
     return jnp.sum(scaled, axis=1)
 
 
-def kernel(
-    msa, pair, g_row, w_row, g_pair, w_bias, wo_row, g_col, w_col, wo_col, g_opm, w_fac, w_fin,
-    out_msa, out_pair,
-    bias_src, bias_in, bias, queries, gates, keys, values, logits, weights, denom, staged, msa_src, msa_in,
-    unpacked, col_src, col_in, col_logits, col_weights, col_denom, natural, final, left_src, left, right_src, right,
-    right_f, final_f, final_w, outer, update, msa_halves, spread,
-    send, recv,
-):
+def kernel(*refs):
+    given, (out_msa, out_pair), held, rest = refs[:13], refs[13:15], refs[15:28], refs[28:]
+    msa, pair, g_row, w_row, g_pair, w_bias, wo_row, g_col, w_col, wo_col, g_opm, w_fac, w_fin = held
+    (
+        bias_src, bias_in, bias, queries, gates, keys, values, logits, weights, denom, staged, msa_src, msa_in,
+        unpacked, col_src, col_in, col_logits, col_weights, col_denom, natural, final, left_src, left, right_src, right,
+        left_f, left_t, outer, update, result_src, result_in, msa_halves, spread,
+        send, recv, load,
+    ) = rest
+    loads = [pltpu.make_async_copy(given[k], held[k], load.at[k]) for k in range(13)]
+    for k in (1, 5, 4, 0, 2, 3, 6, 12, 7, 8, 9, 10, 11):
+        loads[k].start()
+
+    def loaded(*which):
+        for k in which:
+            loads[k].wait()
+
     dap = lax.axis_index("dap")
     rep = lax.axis_index("rep")
     x = dap // 32
@@ -91,7 +100,8 @@
     for step in range(1, 8):
         other = (zh * 4 + rep + step) % 8
         greet(device(xy, other // 4, core), other % 4)
-    greet(device(xy, zh, 1 - core), rep)
+    for step in range(4):
+        greet(device(((x + step) % 4) * 8 + y, zh, 1 - core), rep)
     greet(device(xy, 1 - zh, 1 - core), rep)
     mirror = rep * 8 + y
     greet(device(mirror, 1 - zh, core), x)
@@ -112,32 +122,54 @@
     def drained(shaped, phase):
         pltpu.make_async_copy(shaped, shaped, send.at[phase]).wait()
 
+    leaving = []
+
+    def finish():
+        for shaped, phase in leaving:
+            if shaped is not None:
+                drained(shaped, phase)
+                continue
+
+            @pl.when(x != rep)
+            def _():
+                drained(right.at[0], RIGHT1)
+
+            @pl.when(x == rep)
+            def _():
+                drained(right_src, RIGHT1)
+
     def push_y(buffer, phase):
         for step in range(1, 8):
             block = buffer.at[x, y, core]
             push(block, block, phase, device(x * 8 + (y + step) % 8, zh, core), rep)
+        leaving.append((buffer.at[0, pl.ds(0, 7), 0], phase))
 
     def push_x(buffer, phase):
         for step in range(1, 4):
             block = buffer.at[x, :, core]
             push(block, block, phase, device(((x + step) % 4) * 8 + y, zh, core), rep)
+        leaving.append((buffer.at[pl.ds(0, 3), :, 0], phase))
 
     def push_c(buffer, phase):
         block = buffer.at[:, :, core]
         push(block, block, phase, device(xy, zh, 1 - core), rep)
-
+        leaving.append((buffer.at[:, :, 0], phase))
+
+    loaded(1, 4, 5)
     ln_pair = layer_norm(pair[...].reshape(4 * 128, CZ), g_pair[...])
     head_bias = dot_nt(w_bias[...], ln_pair) * LOG2E
     for a in range(4):
         bias_src[a] = head_bias[:, a * 128 : (a + 1) * 128]
 
-    pl.semaphore_wait(barrier, 41 + jnp.where(x != rep, 1, 0))
+    pl.semaphore_wait(barrier, 44 + jnp.where(x != rep, 1, 0))
 
     for step in range(1, 8):
         other = (zh * 4 + rep + step) % 8
         push(bias_src.at[other % 4], bias_in.at[zh * 4 + rep], BIAS1, device(xy, other // 4, core), other % 4)
+    leaving.append((bias_in.at[pl.ds(0, 7)], BIAS1))
     bias_in[zh * 4 + rep] = bias_src[rep]
 
+    loaded(0, 2, 3)
     for s in range(2):
         tokens = layer_norm(msa[s], g_row[...])
         projected = dot(tokens, w_row[:, FEAT : 3 * FEAT]).astype(BF16)
@@ -168,9 +200,6 @@
     arrived(bias.at[0, pl.ds(0, 7), 0], BIAS_Y)
     push_x(bias, BIAS_X)
     row_logits(1)
-    final_f[...] = w_fin[...].astype(F32)
-    for e in range(FACTOR):
-        final_w[pl.ds(e * FACTOR, FACTOR), :] = final_f[pl.ds(e, FACTOR, stride=FACTOR), :].astype(BF16)
     arrived(bias.at[pl.ds(0, 3), :, 0], BIAS_X)
     push_c(bias, BIAS_C)
 
@@ -189,6 +218,7 @@
     lax.fori_loop(0, 8, row_softmax, core)
     arrived(bias.at[:, :, 0], BIAS_C)
     lax.fori_loop(0, 8, row_softmax, 1 - core)
+    loaded(6)
     for s in range(2):
         attended = dot(weights[s].reshape(1024, RES), values[s])
         merged = merge_heads(attended, denom[s].reshape(1024, 128)[:, :1])
@@ -204,6 +234,7 @@
         return 0
 
     lax.fori_loop(1, 32, push_msa, 0)
+    leaving.append((msa_in.at[pl.ds(0, 31)], MSA1))
     msa_in[xy] = msa_src[xy]
     arrived(msa_in.at[pl.ds(0, 31)], MSA1)
     unpacked[...] = msa_in[...].astype(F32).reshape(512, 128)
@@ -218,9 +249,11 @@
     for step in range(1, 4):
         other = (member + step) % 4
         push(col_src.at[other], col_in.at[member], MSA2, device(xy, other % 2, other // 2), rep)
+    leaving.append((col_in.at[pl.ds(0, 3)], MSA2))
     col_in[member] = col_src[member]
     arrived(col_in.at[pl.ds(0, 3)], MSA2)
 
+    loaded(7, 8, 9, 10, 11, 12)
     middle = col_in[...].astype(F32).reshape(ROWS, FEAT)
     tokens = layer_norm(middle, g_col[...])
     projected = dot(tokens, w_col[...])
@@ -250,19 +283,21 @@
     factors = dot_nt(w_fac[...], ln_opm)
     right_src[...] = factors[FACTOR:].astype(BF16)
     left_src[...] = (factors[:FACTOR] * (1.0 / ROWS)).astype(BF16)
-    push(right_src, right.at[rep, y, core, zh], RIGHT1, device(mirror, 1 - zh, core), x)
+    push(right_src, right.at[y, zh], RIGHT1, device(mirror, 1 - zh, core), x)
 
     @pl.when(x != rep)
     def _():
-        push(right_src, right.at[rep, y, core, zh], RIGHT1, device(mirror, zh, core), x)
+        push(right_src, right.at[y, zh], RIGHT1, device(mirror, zh, core), x)
 
     @pl.when(x == rep)
     def _():
-        right[rep, y, core, zh] = right_src[...]
+        right[y, zh] = right_src[...]
 
     for step in range(1, 4):
-        push(left_src, left.at[rep], LEFT, dap, (rep + step) % 4)
-    left[rep] = left_src[...]
+        push(left_src, left.at[x, core, rep], LEFT, dap, (rep + step) % 4)
+    leaving.append((None, RIGHT1))
+    leaving.append((left.at[0, 0, pl.ds(0, 3)], LEFT))
+    left[x, core, rep] = left_src[...]
     for m_ in range(4):
         for s in range(2):
             start = (m_ * 2 + s) * 32
@@ -273,40 +308,69 @@
     final[rep] = jnp.concatenate([natural[0], natural[1]], axis=1).astype(BF16)
     for step in range(1, 4):
         push(final.at[rep], final.at[rep], FINAL, dap, (rep + step) % 4)
+    leaving.append((final.at[pl.ds(0, 3)], FINAL))
 
     @pl.when(x != rep)
     def _():
-        arrived(right.at[0, 0, 0], RIGHT1)
+        arrived(right.at[0], RIGHT1)
 
     @pl.when(x == rep)
     def _():
         arrived(right_src, RIGHT1)
 
-    push_y(right, RIGHT_Y)
-    arrived(right.at[0, pl.ds(0, 7), 0], RIGHT_Y)
-    push_x(right, RIGHT_X)
-    arrived(right.at[pl.ds(0, 3), :, 0], RIGHT_X)
-    push_c(right, RIGHT_C)
-    arrived(left.at[pl.ds(0, 3)], LEFT)
-    left_all = left[...].reshape(4 * FACTOR, ROWS)
-    arrived(right.at[:, :, 0], RIGHT_C)
+    for step in range(1, 8):
+        push(right.at[y], right.at[y], RIGHT_Y, device(x * 8 + (y + step) % 8, zh, core), rep)
+    leaving.append((right.at[pl.ds(0, 7)], RIGHT_Y))
+    arrived(left.at[0, 0, pl.ds(0, 3)], LEFT)
+    for step in range(1, 4):
+        block = left.at[x, core]
+        push(block, block, LEFT_X, device(((x + step) % 4) * 8 + y, zh, core), rep)
+    leaving.append((left.at[pl.ds(0, 3), 0], LEFT_X))
+    arrived(left.at[pl.ds(0, 3), 0], LEFT_X)
+    block = left.at[:, core]
+    push(block, block, LEFT_C, device(xy, zh, 1 - core), rep)
+    leaving.append((left.at[:, 0], LEFT_C))
+    arrived(left.at[:, 0], LEFT_C)
 
     for half in range(2):
-        right_f[half] = right[..., half * 128 : (half + 1) * 128].astype(F32).reshape(128 * FACTOR, 128)
-    for e in range(FACTOR):
-        operand = jnp.concatenate(
-            [right_f[half, pl.ds(e, 128, stride=FACTOR), :] for half in range(2)], axis=1
+        left_f[half] = left[..., half * 128 : (half + 1) * 128].astype(F32).reshape(32 * FACTOR, 128)
+    for channel in range(FACTOR):
+        left_t[pl.ds(channel * 32, 32), :] = jnp.concatenate(
+            [left_f[half, pl.ds(channel, 32, stride=FACTOR), :] for half in range(2)], axis=1
         ).astype(BF16)
-        product = dot_nt(left_all, operand).astype(BF16)
-        for i in range(4):
-            outer[pl.ds(e * FACTOR, FACTOR), i * 128 : (i + 1) * 128] = product[i * FACTOR : (i + 1) * FACTOR]
-    flat = lax.dot_general(final_w[...], outer[...], (((0,), (0,)), ((), ())), preferred_element_type=F32)
-    for i in range(4):
-        update[i] = flat[:, i * 128 : (i + 1) * 128].T
-        for x_ in range(4):
-            for m_ in range(4):
-                here = pl.ds(8 * (m_ % 2) + 4 * (m_ // 2) + x_, 8, stride=16)
-                out_pair[i, here, :] = pair[i, here, :] + update[i, pl.ds(x_ * 32 + m_, 8, stride=4), :]
+    arrived(right.at[pl.ds(0, 7)], RIGHT_Y)
+    quarter = lax.broadcasted_iota(jnp.int32, (FACTOR, 128), 1) // 32
+    right_all = right[...].reshape(16 * FACTOR, ROWS)
+    for part in range(4):
+        product = dot_nt(right_all, left_t[pl.ds(part * 256, 256), :])
+        for tile in range(2):
+            lanes = slice(tile * 128, (tile + 1) * 128)
+            for four in range(4):
+                blocks = [product[(four * 4 + jq) * FACTOR : (four * 4 + jq + 1) * FACTOR, lanes] for jq in range(4)]
+                for cq in range(4):
+                    moved = [
+                        blocks[jq] if jq == cq else pltpu.roll(blocks[jq], (32 * (jq - cq)) % 128, 1) for jq in range(4)
+                    ]
+                    joined = jnp.where(
+                        quarter < 2,
+                        jnp.where(quarter == 0, moved[0], moved[1]),
+                        jnp.where(quarter == 2, moved[2], moved[3]),
+                    )
+                    channel = part * 8 + tile * 4 + cq
+                    outer[pl.ds(channel * FACTOR, FACTOR), four * 128 : (four + 1) * 128] = joined.astype(BF16)
+    flat = lax.dot_general(w_fin[...], outer[...], (((0,), (0,)), ((), ())), preferred_element_type=F32)
+    for four in range(4):
+        update[pl.ds(four * 128, 128), :] = flat[:, four * 128 : (four + 1) * 128].T
+
+    for target in range(8):
+        for r_ in range(4):
+            result_src[target, r_] = update[pl.ds(target * 4 + r_, 16, stride=32), :].astype(BF16)
+    mine = x * 2 + core
+    for step in range(1, 8):
+        other = (mine + step) % 8
+        push(result_src.at[other], result_in.at[mine], RESULT, device((other // 2) * 8 + y, zh, other % 2), rep)
+    leaving.append((result_in.at[pl.ds(0, 7)], RESULT))
+    result_in[mine] = result_src[mine]
 
     arrived(final.at[pl.ds(0, 3)], FINAL)
     for half in range(2):
@@ -314,26 +378,13 @@
             spread[half, pl.ds(r_, ROWS, stride=4), :] = final[r_, :, half * 128 : (half + 1) * 128].astype(F32)
         out_msa[:, half * 128 : (half + 1) * 128] = spread[half]
 
-    drained(bias_in.at[pl.ds(0, 7)], BIAS1)
-    drained(bias.at[0, pl.ds(0, 7), 0], BIAS_Y)
-    drained(bias.at[pl.ds(0, 3), :, 0], BIAS_X)
-    drained(bias.at[:, :, 0], BIAS_C)
-    drained(msa_in.at[pl.ds(0, 31)], MSA1)
-    drained(col_in.at[pl.ds(0, 3)], MSA2)
-    drained(left.at[pl.ds(0, 3)], LEFT)
-    drained(final.at[pl.ds(0, 3)], FINAL)
-
-    @pl.when(x != rep)
-    def _():
-        drained(right.at[0, 0, 0], RIGHT1)
-
-    @pl.when(x == rep)
-    def _():
-        drained(right_src, RIGHT1)
-
-    drained(right.at[0, pl.ds(0, 7), 0], RIGHT_Y)
-    drained(right.at[pl.ds(0, 3), :, 0], RIGHT_X)
-    drained(right.at[:, :, 0], RIGHT_C)
+    arrived(result_in.at[pl.ds(0, 7)], RESULT)
+    for source in range(8):
+        for a in range(4):
+            here = pl.ds(4 * (source % 2) + source // 2, 16, stride=8)
+            out_pair[a, here, :] = pair[a, here, :] + result_in[source, a].astype(F32)
+
+    finish()
 
 
 def shards(
@@ -351,8 +402,23 @@
     tensorial_factor_matrix,
     tensorial_final_matrix,
 ):
+    operands = [
+        alignment_source_tensor,
+        couple_source_tensor,
+        horizontal_scale_factor.reshape(1, FEAT),
+        horizontal_projection_matrix,
+        couple_scale_factor.reshape(1, CZ),
+        couple_offset_matrix.T,
+        horizontal_final_matrix,
+        vertical_scale_factor.reshape(1, FEAT),
+        vertical_projection_matrix,
+        vertical_final_matrix,
+        tensorial_scale_factor.reshape(1, FEAT),
+        tensorial_factor_matrix.T,
+        tensorial_final_matrix,
+    ]
     vmem = pl.BlockSpec(memory_space=pltpu.VMEM)
-    scratch = [
+    scratch = [pltpu.VMEM(a.shape, a.dtype) for a in operands] + [
         pltpu.VMEM((4, 8, 128), F32),
         pltpu.VMEM((8, 8, 128), F32),
         pltpu.VMEM((4, 8, 2, 16, RES), BF16),
@@ -375,18 +441,20 @@
         pltpu.VMEM((2, ROWS, 128), F32),
         pltpu.VMEM((4, ROWS, FEAT), BF16),
         pltpu.VMEM((FACTOR, ROWS), BF16),
-        pltpu.VMEM((4, FACTOR, ROWS), BF16),
+        pltpu.VMEM((4, 2, 4, FACTOR, ROWS), BF16),
         pltpu.VMEM((FACTOR, ROWS), BF16),
-        pltpu.VMEM((4, 8, 2, 2, FACTOR, ROWS), BF16),
-        pltpu.VMEM((2, 128 * FACTOR, 128), F32),
-        pltpu.VMEM((FACTOR * FACTOR, CZ), F32),
-        pltpu.VMEM((FACTOR * FACTOR, CZ), BF16),
+        pltpu.VMEM((8, 2, FACTOR, ROWS), BF16),
+        pltpu.VMEM((2, 32 * FACTOR, 128), F32),
+        pltpu.VMEM((32 * FACTOR, ROWS), BF16),
         pltpu.VMEM((FACTOR * FACTOR, 512), BF16),
-        pltpu.VMEM((4, 128, CZ), F32),
+        pltpu.VMEM((512, CZ), F32),
+        pltpu.VMEM((8, 4, 16, CZ), BF16),
+        pltpu.VMEM((8, 4, 16, CZ), BF16),
         pltpu.VMEM((2, 2, RES, 128), F32),
         pltpu.VMEM((2, ROWS * 4, 128), F32),
         pltpu.SemaphoreType.DMA((PHASES,)),
         pltpu.SemaphoreType.DMA((PHASES,)),
+        pltpu.SemaphoreType.DMA((len(operands),)),
     ]
     out_msa, out_pair = pl.pallas_call(
         kernel,
@@ -394,27 +462,13 @@
             jax.ShapeDtypeStruct((ROWS * 4, FEAT), F32),
             jax.ShapeDtypeStruct((4, 128, CZ), F32),
         ),
-        in_specs=[vmem] * 13,
+        in_specs=[pl.BlockSpec(memory_space=pltpu.HBM)] * len(operands),
         out_specs=(vmem, vmem),
         scratch_shapes=scratch,
         compiler_params=pltpu.CompilerParams(
-            collective_id=0, has_side_effects=True, vmem_limit_bytes=48 * 1024 * 1024
+            collective_id=0, has_side_effects=True, vmem_limit_bytes=60 * 1024 * 1024
         ),
-    )(
-        alignment_source_tensor,
-        couple_source_tensor,
-        horizontal_scale_factor.reshape(1, FEAT),
-        horizontal_projection_matrix,
-        couple_scale_factor.reshape(1, CZ),
-        couple_offset_matrix.T,
-        horizontal_final_matrix,
-        vertical_scale_factor.reshape(1, FEAT),
-        vertical_projection_matrix,
-        vertical_final_matrix,
-        tensorial_scale_factor.reshape(1, FEAT),
-        tensorial_factor_matrix.T,
-        tensorial_final_matrix,
-    )
+    )(*operands)
     return out_msa.reshape(ROWS, 4, FEAT), out_pair
 
 

time: 99.9 us -> 85.2 us (0.85)
  Pallas kernels: 88.3 us -> 81.1 us
  local copies, waits for them, and re-layouts: 10.4 us -> 3.25 us
    unnamed x27 -> x3, local copies, waits for them, and re-layouts: 9.16 us -> 0.71 us
    pallas_call x1, Pallas kernels: 88.3 us -> 81.1 us  [shards(): pl.pallas_call(kernel, out_shape=(jax.ShapeDtypeStruct((ROWS * 4, FEAT),...]
    reshape x1, local copies, waits for them, and re-layouts: 1.27 us -> 2.54 us  [shards(): return (out_msa.reshape(ROWS, 4, FEAT), out_pair)]
where the time goes in v2:
time: 85.2 us; the launch traced here: 85 us
  Pallas kernels  81.1 us (95%)
  local copies, waits for them, and re-layouts  3.25 us (4%)
    pallas_call x1, Pallas kernels, shards(): pl.pallas_call(kernel, out_shape=(jax.ShapeDtypeStruct((ROWS * 4, FEAT),...  81.1 us
    reshape x1, local copies, waits for them, and re-layouts, shards(): return (out_msa.reshape(ROWS, 4, FEAT), out_pair)  2.54 us

profile of v2, /device:TPU:1, one launch (start us, length us, event | category | flops | bytes accessed | tf_op | source)
XLA Modules:
  0.0 85.0 jit_solution(1038949393539556074)
XLA Ops:
  0.6 81.1 %shard_map.140 = (f32[1024,256]{1,0:T(8,128)}, f32[4,128,128]{2,1,0:T(8,128)}) custom-call(f32[2,512,256]{2,1,0:T(8,128)} %refs_0_.1, f32[4,128,128]{2,1,0:T(8,128)} %refs_1_.1, f32[1,256]{1,0:T(1,128)} %bitcast.8, bf16[256,1024]{1,0:T(8,128)(2,1)} %refs_3_.1, f32[1,128]{1,0:T(1,128)} %bitcast.11, bf16[8,128]{1,0:T(8,128)(2,1)} %bitcast.7, ...), custom_call_target="tpu_custom_call" | custom-call | tf_op jit(solution)/shard_map/pallas_call | solution.py:459
  81.7 0.0 copy-start
  81.8 2.5 %reshape.23 = f32[256,4,256]{2,1,0:T(4,128)} reshape(f32[1024,256]{1,0:T(8,128)} %get-tuple-element.4) | data formatting | bytes 2097152 | tf_op jit(solution)/shard_map/reshape | solution.py:472
  84.3 0.0 copy-done
  84.3 0.7 copy.16
Async XLA Ops:
  81.7 2.6 %copy-start = (f32[4,128,128]{2,1,0:T(8,128)S(1)}, f32[4,128,128]{2,1,0:T(8,128)}, u32[]{:S(2)}) copy-start(f32[4,128,128]{2,1,0:T(8,128)} %get-tuple-element.9) | copy-start | bytes 786436

commit v3 on v2

--- a/solution.py
+++ b/solution.py
@@ -64,7 +64,7 @@
         bias_src, bias_in, bias, queries, gates, keys, values, logits, weights, denom, staged, msa_src, msa_in,
         unpacked, col_src, col_in, col_logits, col_weights, col_denom, natural, final, left_src, left, right_src, right,
         left_f, left_t, outer, update, result_src, result_in, msa_halves, spread,
-        send, recv, load,
+        send, recv, load, recv_by, recv_bx, recv_r1,
     ) = rest
     loads = [pltpu.make_async_copy(given[k], held[k], load.at[k]) for k in range(13)]
     for k in (1, 5, 4, 0, 2, 3, 6, 12, 7, 8, 9, 10, 11):
@@ -110,14 +110,17 @@
     def _():
         greet(device(mirror, zh, core), x)
 
-    def push(src, dst, phase, dap_, rep_):
+    def push(src, dst, phase, dap_, rep_, into=None):
         pltpu.make_async_remote_copy(
-            src_ref=src, dst_ref=dst, send_sem=send.at[phase], recv_sem=recv.at[phase],
+            src_ref=src, dst_ref=dst, send_sem=send.at[phase], recv_sem=recv.at[phase] if into is None else into,
             device_id=(dap_, rep_), device_id_type=MESH,
         ).start()
 
     def arrived(shaped, phase):
-        pltpu.make_async_copy(shaped, shaped, recv.at[phase]).wait()
+        landed(shaped, recv.at[phase])
+
+    def landed(shaped, sem):
+        pltpu.make_async_copy(shaped, shaped, sem).wait()
 
     def drained(shaped, phase):
         pltpu.make_async_copy(shaped, shaped, send.at[phase]).wait()
@@ -138,22 +141,14 @@
             def _():
                 drained(right_src, RIGHT1)
 
-    def push_y(buffer, phase):
-        for step in range(1, 8):
-            block = buffer.at[x, y, core]
-            push(block, block, phase, device(x * 8 + (y + step) % 8, zh, core), rep)
-        leaving.append((buffer.at[0, pl.ds(0, 7), 0], phase))
-
-    def push_x(buffer, phase):
+    def bias_along_x(y_):
+        block = bias.at[x, y_, core]
         for step in range(1, 4):
-            block = buffer.at[x, :, core]
-            push(block, block, phase, device(((x + step) % 4) * 8 + y, zh, core), rep)
-        leaving.append((buffer.at[pl.ds(0, 3), :, 0], phase))
-
-    def push_c(buffer, phase):
-        block = buffer.at[:, :, core]
-        push(block, block, phase, device(xy, zh, 1 - core), rep)
-        leaving.append((buffer.at[:, :, 0], phase))
+            push(block, block, BIAS_X, device(((x + step) % 4) * 8 + y, zh, core), rep, recv_bx.at[x * 8 + y_])
+
+    def bias_to_core(y_):
+        block = bias.at[:, y_, core]
+        push(block, block, BIAS_C, device(xy, zh, 1 - core), rep)
 
     loaded(1, 4, 5)
     ln_pair = layer_norm(pair[...].reshape(4 * 128, CZ), g_pair[...])
@@ -188,7 +183,10 @@
         [jnp.concatenate([bias_in[h_ * 4 + r_] for r_ in range(4)], axis=1) for h_ in range(2)], axis=0
     )
     bias[x, y, core] = block.astype(BF16)
-    push_y(bias, BIAS_Y)
+    for step in (4, 3, 5, 2, 6, 1, 7):
+        block = bias.at[x, y, core]
+        push(block, block, BIAS_Y, device(x * 8 + (y + step) % 8, zh, core), rep, recv_by.at[y])
+    bias_along_x(y)
 
     def row_logits(s):
         tokens = layer_norm(jnp.concatenate([queries[s, 0], queries[s, 1]], axis=1), g_row[...])
@@ -197,11 +195,19 @@
         logits[s] = dot_nt(expand_heads(wide), keys[s]).reshape(32, 2, 16, RES)
 
     row_logits(0)
-    arrived(bias.at[0, pl.ds(0, 7), 0], BIAS_Y)
-    push_x(bias, BIAS_X)
+    for step in (1, 7, 2, 6, 3, 5, 4):
+        source = (y + step) % 8
+        landed(bias.at[0, 0, 0], recv_by.at[source])
+        bias_along_x(source)
     row_logits(1)
-    arrived(bias.at[pl.ds(0, 3), :, 0], BIAS_X)
-    push_c(bias, BIAS_C)
+    for step in (0, 1, 7, 2, 6, 3, 5, 4):
+        source = (y + step) % 8
+        for other in range(1, 4):
+            landed(bias.at[0, 0, 0], recv_bx.at[((x + other) % 4) * 8 + source])
+        bias_to_core(source)
+    leaving.append((bias.at[0, pl.ds(0, 7), 0], BIAS_Y))
+    leaving.append((bias.at[pl.ds(0, 3), :, 0], BIAS_X))
+    leaving.append((bias.at[:, :, 0], BIAS_C))
 
     def row_softmax(group, which):
         rows = pl.ds(group * 4, 4)
@@ -283,11 +289,11 @@
     factors = dot_nt(w_fac[...], ln_opm)
     right_src[...] = factors[FACTOR:].astype(BF16)
     left_src[...] = (factors[:FACTOR] * (1.0 / ROWS)).astype(BF16)
-    push(right_src, right.at[y, zh], RIGHT1, device(mirror, 1 - zh, core), x)
+    push(right_src, right.at[y, zh], RIGHT1, device(mirror, 1 - zh, core), x, recv_r1.at[zh])
 
     @pl.when(x != rep)
     def _():
-        push(right_src, right.at[y, zh], RIGHT1, device(mirror, zh, core), x)
+        push(right_src, right.at[y, zh], RIGHT1, device(mirror, zh, core), x, recv_r1.at[zh])
 
     @pl.when(x == rep)
     def _():
@@ -306,26 +312,27 @@
                     start : start + 32, half * 128 : (half + 1) * 128
                 ]
     final[rep] = jnp.concatenate([natural[0], natural[1]], axis=1).astype(BF16)
+    def right_along_y(zh_):
+        for step in (4, 3, 5, 2, 6, 1, 7):
+            block = right.at[y, zh_]
+            push(block, block, RIGHT_Y, device(x * 8 + (y + step) % 8, zh, core), rep)
+
+    @pl.when(x != rep)
+    def _():
+        landed(right_src, recv_r1.at[zh])
+
+    right_along_y(zh)
+    arrived(left.at[0, 0, pl.ds(0, 3)], LEFT)
+    for step in (2, 1, 3):
+        block = left.at[x, core]
+        push(block, block, LEFT_X, device(((x + step) % 4) * 8 + y, zh, core), rep)
+    leaving.append((left.at[pl.ds(0, 3), 0], LEFT_X))
+    landed(right_src, recv_r1.at[1 - zh])
+    right_along_y(1 - zh)
+    leaving.append((right.at[pl.ds(0, 7)], RIGHT_Y))
     for step in range(1, 4):
         push(final.at[rep], final.at[rep], FINAL, dap, (rep + step) % 4)
     leaving.append((final.at[pl.ds(0, 3)], FINAL))
-
-    @pl.when(x != rep)
-    def _():
-        arrived(right.at[0], RIGHT1)
-
-    @pl.when(x == rep)
-    def _():
-        arrived(right_src, RIGHT1)
-
-    for step in range(1, 8):
-        push(right.at[y], right.at[y], RIGHT_Y, device(x * 8 + (y + step) % 8, zh, core), rep)
-    leaving.append((right.at[pl.ds(0, 7)], RIGHT_Y))
-    arrived(left.at[0, 0, pl.ds(0, 3)], LEFT)
-    for step in range(1, 4):
-        block = left.at[x, core]
-        push(block, block, LEFT_X, device(((x + step) % 4) * 8 + y, zh, core), rep)
-    leaving.append((left.at[pl.ds(0, 3), 0], LEFT_X))
     arrived(left.at[pl.ds(0, 3), 0], LEFT_X)
     block = left.at[:, core]
     push(block, block, LEFT_C, device(xy, zh, 1 - core), rep)
@@ -455,6 +462,9 @@
         pltpu.SemaphoreType.DMA((PHASES,)),
         pltpu.SemaphoreType.DMA((PHASES,)),
         pltpu.SemaphoreType.DMA((len(operands),)),
+        pltpu.SemaphoreType.DMA((8,)),
+        pltpu.SemaphoreType.DMA((32,)),
+        pltpu.SemaphoreType.DMA((2,)),
     ]
     out_msa, out_pair = pl.pallas_call(
         kernel,

time: 85.2 us -> 77.4 us (0.908)
  Pallas kernels: 81.1 us -> 73.4 us
    pallas_call x1, Pallas kernels: 81.1 us -> 73.4 us  [shards(): pl.pallas_call(kernel, out_shape=(jax.ShapeDtypeStruct((ROWS * 4, FEAT),...]
where the time goes in v3:
time: 77.4 us; the launch traced here: 77.3 us
  Pallas kernels  73.4 us (95%)
  local copies, waits for them, and re-layouts  3.25 us (4%)
    pallas_call x1, Pallas kernels, shards(): pl.pallas_call(kernel, out_shape=(jax.ShapeDtypeStruct((ROWS * 4, FEAT),...  73.4 us
    reshape x1, local copies, waits for them, and re-layouts, shards(): return (out_msa.reshape(ROWS, 4, FEAT), out_pair)  2.54 us

profile of v3, /device:TPU:1, one launch (start us, length us, event | category | flops | bytes accessed | tf_op | source)
XLA Modules:
  0.0 77.3 jit_solution(11920416068292054428)
XLA Ops:
  0.6 73.4 %shard_map.140 = (f32[1024,256]{1,0:T(8,128)}, f32[4,128,128]{2,1,0:T(8,128)}) custom-call(f32[2,512,256]{2,1,0:T(8,128)} %refs_0_.1, f32[4,128,128]{2,1,0:T(8,128)} %refs_1_.1, f32[1,256]{1,0:T(1,128)} %bitcast.8, bf16[256,1024]{1,0:T(8,128)(2,1)} %refs_3_.1, f32[1,128]{1,0:T(1,128)} %bitcast.11, bf16[8,128]{1,0:T(8,128)(2,1)} %bitcast.7, ...), custom_call_target="tpu_custom_call" | custom-call | tf_op jit(solution)/shard_map/pallas_call | solution.py:469
  74.0 0.0 copy-start
  74.0 2.5 %reshape.23 = f32[256,4,256]{2,1,0:T(4,128)} reshape(f32[1024,256]{1,0:T(8,128)} %get-tuple-element.4) | data formatting | bytes 2097152 | tf_op jit(solution)/shard_map/reshape | solution.py:482
  76.6 0.0 copy-done
  76.6 0.7 copy.16
Async XLA Ops:
  74.0 2.6 %copy-start = (f32[4,128,128]{2,1,0:T(8,128)S(1)}, f32[4,128,128]{2,1,0:T(8,128)}, u32[]{:S(2)}) copy-start(f32[4,128,128]{2,1,0:T(8,128)} %get-tuple-element.9) | copy-start | bytes 786436

commit v4 on v3

--- a/solution.py
+++ b/solution.py
@@ -63,11 +63,11 @@
     (
         bias_src, bias_in, bias, queries, gates, keys, values, logits, weights, denom, staged, msa_src, msa_in,
         unpacked, col_src, col_in, col_logits, col_weights, col_denom, natural, final, left_src, left, right_src, right,
-        left_f, left_t, outer, update, result_src, result_in, msa_halves, spread,
-        send, recv, load, recv_by, recv_bx, recv_r1,
+        left_f, left_t, outer, update, result_src, result_in, msa_halves,
+        send, recv, load, recv_by, recv_bx, recv_bc, recv_r1,
     ) = rest
     loads = [pltpu.make_async_copy(given[k], held[k], load.at[k]) for k in range(13)]
-    for k in (1, 5, 4, 0, 2, 3, 6, 12, 7, 8, 9, 10, 11):
+    for k in (1, 5, 4):
         loads[k].start()
 
     def loaded(*which):
@@ -82,7 +82,6 @@
     zc = dap % 4
     zh = zc // 2
     core = zc % 2
-    member = core * 2 + zh
 
     def device(xy_, zh_, core_):
         return xy_ * 4 + zh_ * 2 + core_
@@ -92,23 +91,29 @@
     def greet(dap_, rep_):
         pl.semaphore_signal(barrier, inc=1, device_id=(dap_, rep_), device_id_type=MESH)
 
-    def greet_xy(step, _):
-        greet(device((xy + step) % 32, zh, core), rep)
+    def far_first(turn):
+        return (xy + (turn + 11) % 31 + 1) % 32
+
+    def greet_xy(turn, _):
+        greet(device(far_first(turn), zh, core), rep)
         return 0
 
-    lax.fori_loop(1, 32, greet_xy, 0)
-    for step in range(1, 8):
+    mirror = rep * 8 + y
+    greet(device(mirror, 1 - zh, core), x)
+
+    @pl.when(x != rep)
+    def _():
+        greet(device(mirror, zh, core), x)
+
+    lax.fori_loop(0, 31, greet_xy, 0)
+    for step in (4, 3, 5, 2, 6, 1, 7):
         other = (zh * 4 + rep + step) % 8
         greet(device(xy, other // 4, core), other % 4)
     for step in range(4):
         greet(device(((x + step) % 4) * 8 + y, zh, 1 - core), rep)
     greet(device(xy, 1 - zh, 1 - core), rep)
-    mirror = rep * 8 + y
-    greet(device(mirror, 1 - zh, core), x)
-
-    @pl.when(x != rep)
-    def _():
-        greet(device(mirror, zh, core), x)
+    for k in (0, 2, 3, 6, 12, 7, 8, 9, 10, 11):
+        loads[k].start()
 
     def push(src, dst, phase, dap_, rep_, into=None):
         pltpu.make_async_remote_copy(
@@ -148,7 +153,7 @@
 
     def bias_to_core(y_):
         block = bias.at[:, y_, core]
-        push(block, block, BIAS_C, device(xy, zh, 1 - core), rep)
+        push(block, block, BIAS_C, device(xy, zh, 1 - core), rep, recv_bc.at[y_])
 
     loaded(1, 4, 5)
     ln_pair = layer_norm(pair[...].reshape(4 * 128, CZ), g_pair[...])
@@ -158,7 +163,7 @@
 
     pl.semaphore_wait(barrier, 44 + jnp.where(x != rep, 1, 0))
 
-    for step in range(1, 8):
+    for step in (4, 3, 5, 2, 6, 1, 7):
         other = (zh * 4 + rep + step) % 8
         push(bias_src.at[other % 4], bias_in.at[zh * 4 + rep], BIAS1, device(xy, other // 4, core), other % 4)
     leaving.append((bias_in.at[pl.ds(0, 7)], BIAS1))
@@ -174,7 +179,7 @@
             msa_halves[s, half] = msa[s, :, half * 128 : (half + 1) * 128]
             for h_ in range(2):
                 for c_ in range(2):
-                    queries[s, half, pl.ds(c_ * 2 + h_, 32, stride=4), :] = msa_halves[
+                    queries[s, c_, half, pl.ds(h_, 32, stride=2), :] = msa_halves[
                         s, half, pl.ds(8 * h_ + 4 * c_ + rep, 32, stride=16), :
                     ]
 
@@ -189,10 +194,36 @@
     bias_along_x(y)
 
     def row_logits(s):
-        tokens = layer_norm(jnp.concatenate([queries[s, 0], queries[s, 1]], axis=1), g_row[...])
+        halves = [jnp.concatenate([queries[s, 0, half], queries[s, 1, half]], axis=0) for half in range(2)]
+        tokens = layer_norm(jnp.concatenate(halves, axis=1), g_row[...])
         wide = dot(tokens, w_row[:, :FEAT]) * LOGIT_SCALE
-        gates[s] = jax.nn.sigmoid(dot(tokens, w_row[:, 3 * FEAT :]))
-        logits[s] = dot_nt(expand_heads(wide), keys[s]).reshape(32, 2, 16, RES)
+        gates[s] = jax.nn.sigmoid(dot(tokens, w_row[:, 3 * FEAT :])).reshape(2, 64, FEAT)
+        logits[s] = dot_nt(expand_heads(wide), keys[s]).reshape(2, 4, 8, 16, RES)
+
+    def nearest(turn):
+        away = (turn + 1) // 2
+        return (y + jnp.where(turn % 2 == 1, away, 8 - away)) % 8
+
+    def row_softmax(y_, which):
+        offset = bias[:, y_, which].astype(F32).reshape(64, RES)
+        for s in range(2):
+            raw = logits[s, which, :, y_].reshape(64, RES) + offset
+            top = jnp.max(raw, axis=-1, keepdims=True)
+            powers = jnp.exp2(raw - top)
+            total = jnp.sum(powers, axis=-1, keepdims=True)
+            weights[s, which, :, y_] = powers.astype(BF16).reshape(4, 16, RES)
+            denom[s, which, :, y_] = jnp.broadcast_to(1.0 / total, (64, 128)).reshape(4, 16, 128)
+
+    def row_finish(which):
+        for s in range(2):
+            attended = dot(weights[s, which].reshape(512, RES), values[s])
+            merged = merge_heads(attended, denom[s, which].reshape(512, 128)[:, :1])
+            gated = (merged * gates[s, which]).astype(BF16)
+            change = dot(gated, wo_row[...])
+            for half in range(2):
+                staged[pl.ds(which * 4 + s * 2 + half, 64, stride=8), :] = (
+                    queries[s, which, half] + change[:, half * 128 : (half + 1) * 128]
+                )
 
     row_logits(0)
     for step in (1, 7, 2, 6, 3, 5, 4):
@@ -200,46 +231,37 @@
         landed(bias.at[0, 0, 0], recv_by.at[source])
         bias_along_x(source)
     row_logits(1)
-    for step in (0, 1, 7, 2, 6, 3, 5, 4):
-        source = (y + step) % 8
+
+    def own_queries(turn, _):
+        source = nearest(turn)
         for other in range(1, 4):
             landed(bias.at[0, 0, 0], recv_bx.at[((x + other) % 4) * 8 + source])
         bias_to_core(source)
+        row_softmax(source, core)
+        return 0
+
+    def other_queries(turn, _):
+        source = nearest(turn)
+        landed(bias.at[:, 0, 0], recv_bc.at[source])
+        row_softmax(source, 1 - core)
+        return 0
+
+    loaded(6)
+    lax.fori_loop(0, 8, own_queries, 0)
+    row_finish(core)
+    lax.fori_loop(0, 8, other_queries, 0)
+    row_finish(1 - core)
     leaving.append((bias.at[0, pl.ds(0, 7), 0], BIAS_Y))
     leaving.append((bias.at[pl.ds(0, 3), :, 0], BIAS_X))
     leaving.append((bias.at[:, :, 0], BIAS_C))
-
-    def row_softmax(group, which):
-        rows = pl.ds(group * 4, 4)
-        offset = bias[group // 2, pl.ds((group % 2) * 4, 4), which].astype(F32).reshape(64, RES)
-        for s in range(2):
-            raw = logits[s, rows, which].reshape(64, RES) + offset
-            top = jnp.max(raw, axis=-1, keepdims=True)
-            powers = jnp.exp2(raw - top)
-            total = jnp.sum(powers, axis=-1, keepdims=True)
-            weights[s, rows, which] = powers.astype(BF16).reshape(4, 16, RES)
-            denom[s, rows, which] = jnp.broadcast_to(1.0 / total, (64, 128)).reshape(4, 16, 128)
-        return which
-
-    lax.fori_loop(0, 8, row_softmax, core)
-    arrived(bias.at[:, :, 0], BIAS_C)
-    lax.fori_loop(0, 8, row_softmax, 1 - core)
-    loaded(6)
-    for s in range(2):
-        attended = dot(weights[s].reshape(1024, RES), values[s])
-        merged = merge_heads(attended, denom[s].reshape(1024, 128)[:, :1])
-        gated = (merged * gates[s]).astype(BF16)
-        change = dot(gated, wo_row[...])
-        for half in range(2):
-            staged[pl.ds(s * 2 + half, 128, stride=4), :] = queries[s, half] + change[:, half * 128 : (half + 1) * 128]
     msa_src[...] = staged[...].astype(BF16).reshape(32, 16, 128)
 
-    def push_msa(step, _):
-        other = (xy + step) % 32
+    def push_msa(turn, _):
+        other = far_first(turn)
         push(msa_src.at[other], msa_in.at[xy], MSA1, device(other, zh, core), rep)
         return 0
 
-    lax.fori_loop(1, 32, push_msa, 0)
+    lax.fori_loop(0, 31, push_msa, 0)
     leaving.append((msa_in.at[pl.ds(0, 31)], MSA1))
     msa_in[xy] = msa_src[xy]
     arrived(msa_in.at[pl.ds(0, 31)], MSA1)
@@ -253,10 +275,10 @@
         ]
         col_src[target] = jnp.concatenate(parts, axis=0).astype(BF16)
     for step in range(1, 4):
-        other = (member + step) % 4
-        push(col_src.at[other], col_in.at[member], MSA2, device(xy, other % 2, other // 2), rep)
+        other = (zc + step) % 4
+        push(col_src.at[other], col_in.at[zc], MSA2, device(xy, other // 2, other % 2), rep)
     leaving.append((col_in.at[pl.ds(0, 3)], MSA2))
-    col_in[member] = col_src[member]
+    col_in[zc] = col_src[zc]
     arrived(col_in.at[pl.ds(0, 3)], MSA2)
 
     loaded(7, 8, 9, 10, 11, 12)
@@ -308,7 +330,7 @@
         for s in range(2):
             start = (m_ * 2 + s) * 32
             for half in range(2):
-                natural[half, pl.ds((m_ % 2) * 4 + (m_ // 2) * 2 + s, 32, stride=8), :] = target_rows[
+                natural[half, pl.ds(m_ * 2 + s, 32, stride=8), :] = target_rows[
                     start : start + 32, half * 128 : (half + 1) * 128
                 ]
     final[rep] = jnp.concatenate([natural[0], natural[1]], axis=1).astype(BF16)
@@ -382,8 +404,7 @@
     arrived(final.at[pl.ds(0, 3)], FINAL)
     for half in range(2):
         for r_ in range(4):
-            spread[half, pl.ds(r_, ROWS, stride=4), :] = final[r_, :, half * 128 : (half + 1) * 128].astype(F32)
-        out_msa[:, half * 128 : (half + 1) * 128] = spread[half]
+            out_msa[pl.ds(half * 4 + r_, ROWS, stride=8), :] = final[r_, :, half * 128 : (half + 1) * 128].astype(F32)
 
     arrived(result_in.at[pl.ds(0, 7)], RESULT)
     for source in range(8):
@@ -429,13 +450,13 @@
         pltpu.VMEM((4, 8, 128), F32),
         pltpu.VMEM((8, 8, 128), F32),
         pltpu.VMEM((4, 8, 2, 16, RES), BF16),
-        pltpu.VMEM((2, 2, 128, 128), F32),
-        pltpu.VMEM((2, 128, FEAT), F32),
+        pltpu.VMEM((2, 2, 2, 64, 128), F32),
+        pltpu.VMEM((2, 2, 64, FEAT), F32),
         pltpu.VMEM((2, RES, FEAT), BF16),
         pltpu.VMEM((2, RES, FEAT), BF16),
-        pltpu.VMEM((2, 32, 2, 16, RES), F32),
-        pltpu.VMEM((2, 32, 2, 16, RES), BF16),
-        pltpu.VMEM((2, 32, 2, 16, 128), F32),
+        pltpu.VMEM((2, 2, 4, 8, 16, RES), F32),
+        pltpu.VMEM((2, 2, 4, 8, 16, RES), BF16),
+        pltpu.VMEM((2, 2, 4, 8, 16, 128), F32),
         pltpu.VMEM((512, 128), F32),
         pltpu.VMEM((32, 16, 128), BF16),
         pltpu.VMEM((32, 16, 128), BF16),
@@ -458,18 +479,18 @@
         pltpu.VMEM((8, 4, 16, CZ), BF16),
         pltpu.VMEM((8, 4, 16, CZ), BF16),
         pltpu.VMEM((2, 2, RES, 128), F32),
-        pltpu.VMEM((2, ROWS * 4, 128), F32),
         pltpu.SemaphoreType.DMA((PHASES,)),
         pltpu.SemaphoreType.DMA((PHASES,)),
         pltpu.SemaphoreType.DMA((len(operands),)),
         pltpu.SemaphoreType.DMA((8,)),
         pltpu.SemaphoreType.DMA((32,)),
+        pltpu.SemaphoreType.DMA((8,)),
         pltpu.SemaphoreType.DMA((2,)),
     ]
     out_msa, out_pair = pl.pallas_call(
         kernel,
         out_shape=(
-            jax.ShapeDtypeStruct((ROWS * 4, FEAT), F32),
+            jax.ShapeDtypeStruct((ROWS * 8, 128), F32),
             jax.ShapeDtypeStruct((4, 128, CZ), F32),
         ),
         in_specs=[pl.BlockSpec(memory_space=pltpu.HBM)] * len(operands),
@@ -479,7 +500,7 @@
             collective_id=0, has_side_effects=True, vmem_limit_bytes=60 * 1024 * 1024
         ),
     )(*operands)
-    return out_msa.reshape(ROWS, 4, FEAT), out_pair
+    return jnp.swapaxes(out_msa.reshape(ROWS, 2, 4, 128), 1, 2).reshape(ROWS, 4, FEAT), out_pair
 
 
 def solution(mesh):

time: 77.4 us -> 76.5 us (0.988)
  Pallas kernels: 73.4 us -> 72.6 us
    reshape x1 -> x0, local copies, waits for them, and re-layouts: 2.54 us -> none  [shards(): return (out_msa.reshape(ROWS, 4, FEAT), out_pair)]
    unnamed x3 -> x4, local copies, waits for them, and re-layouts: 0.71 us -> 3.12 us
    pallas_call x1, Pallas kernels: 73.4 us -> 72.6 us  [shards(): pl.pallas_call(kernel, out_shape=(jax.ShapeDtypeStruct((ROWS * 8, 128), F...]
where the time goes in v4:
time: 76.5 us; the launch traced here: 76.4 us
  Pallas kernels  72.6 us (95%)
  local copies, waits for them, and re-layouts  3.12 us (4%)
    pallas_call x1, Pallas kernels, shards(): pl.pallas_call(kernel, out_shape=(jax.ShapeDtypeStruct((ROWS * 8, 128), F...  72.6 us
    unnamed x4, local copies, waits for them, and re-layouts  3.12 us

profile of v4, /device:TPU:1, one launch (start us, length us, event | category | flops | bytes accessed | tf_op | source)
XLA Modules:
  0.0 76.4 jit_solution(830554624654557682)
XLA Ops:
  0.6 72.6 %shard_map.140 = (f32[2048,128]{1,0:T(8,128)}, f32[4,128,128]{2,1,0:T(8,128)}) custom-call(f32[2,512,256]{2,1,0:T(8,128)} %refs_0_.1, f32[4,128,128]{2,1,0:T(8,128)} %refs_1_.1, f32[1,256]{1,0:T(1,128)} %bitcast.14, bf16[256,1024]{1,0:T(8,128)(2,1)} %refs_3_.1, f32[1,128]{1,0:T(1,128)} %bitcast.17, bf16[8,128]{1,0:T(8,128)(2,1)} %bitcast.13, ...), custom_call_target="tpu_custom_call" | custom-call | tf_op jit(solution)/shard_map/pallas_call | solution.py:490
  73.2 0.0 copy-start
  73.2 2.4 %copy.18 = f32[256,4,256]{2,1,0:T(4,128)} copy(f32[256,4,256]{2,1,0:T(4,128)} %bitcast.11) | data formatting | bytes 2097152
  75.6 0.0 copy-done
  75.7 0.7 copy.19
Async XLA Ops:
  73.2 2.4 %copy-start = (f32[4,128,128]{2,1,0:T(8,128)S(1)}, f32[4,128,128]{2,1,0:T(8,128)}, u32[]{:S(2)}) copy-start(f32[4,128,128]{2,1,0:T(8,128)} %get-tuple-element.9) | copy-start | bytes 786436

commit v5 on v4

--- a/solution.py
+++ b/solution.py
@@ -63,8 +63,8 @@
     (
         bias_src, bias_in, bias, queries, gates, keys, values, logits, weights, denom, staged, msa_src, msa_in,
         unpacked, col_src, col_in, col_logits, col_weights, col_denom, natural, final, left_src, left, right_src, right,
-        left_f, left_t, outer, update, result_src, result_in, msa_halves,
-        send, recv, load, recv_by, recv_bx, recv_bc, recv_r1,
+        left_f, left_t, final_t, outer, update, result_src, result_in, msa_halves,
+        send, recv, load, recv_by, recv_bx, recv_bc, recv_r1, recv_ry,
     ) = rest
     loads = [pltpu.make_async_copy(given[k], held[k], load.at[k]) for k in range(13)]
     for k in (1, 5, 4):
@@ -76,12 +76,12 @@
 
     dap = lax.axis_index("dap")
     rep = lax.axis_index("rep")
-    x = dap // 32
-    y = (dap // 4) % 8
-    xy = dap // 4
-    zc = dap % 4
-    zh = zc // 2
-    core = zc % 2
+    x = dap >> 5
+    y = (dap >> 2) & 7
+    xy = dap >> 2
+    zc = dap & 3
+    zh = zc >> 1
+    core = zc & 1
 
     def device(xy_, zh_, core_):
         return xy_ * 4 + zh_ * 2 + core_
@@ -92,7 +92,7 @@
         pl.semaphore_signal(barrier, inc=1, device_id=(dap_, rep_), device_id_type=MESH)
 
     def far_first(turn):
-        return (xy + (turn + 11) % 31 + 1) % 32
+        return (xy + turn + jnp.where(turn < 20, 12, -19)) & 31
 
     def greet_xy(turn, _):
         greet(device(far_first(turn), zh, core), rep)
@@ -107,10 +107,10 @@
 
     lax.fori_loop(0, 31, greet_xy, 0)
     for step in (4, 3, 5, 2, 6, 1, 7):
-        other = (zh * 4 + rep + step) % 8
-        greet(device(xy, other // 4, core), other % 4)
+        other = (zh * 4 + rep + step) & 7
+        greet(device(xy, other >> 2, core), other & 3)
     for step in range(4):
-        greet(device(((x + step) % 4) * 8 + y, zh, 1 - core), rep)
+        greet(device(((x + step) & 3) * 8 + y, zh, 1 - core), rep)
     greet(device(xy, 1 - zh, 1 - core), rep)
     for k in (0, 2, 3, 6, 12, 7, 8, 9, 10, 11):
         loads[k].start()
@@ -149,7 +149,7 @@
     def bias_along_x(y_):
         block = bias.at[x, y_, core]
         for step in range(1, 4):
-            push(block, block, BIAS_X, device(((x + step) % 4) * 8 + y, zh, core), rep, recv_bx.at[x * 8 + y_])
+            push(block, block, BIAS_X, device(((x + step) & 3) * 8 + y, zh, core), rep, recv_bx.at[x * 8 + y_])
 
     def bias_to_core(y_):
         block = bias.at[:, y_, core]
@@ -164,8 +164,8 @@
     pl.semaphore_wait(barrier, 44 + jnp.where(x != rep, 1, 0))
 
     for step in (4, 3, 5, 2, 6, 1, 7):
-        other = (zh * 4 + rep + step) % 8
-        push(bias_src.at[other % 4], bias_in.at[zh * 4 + rep], BIAS1, device(xy, other // 4, core), other % 4)
+        other = (zh * 4 + rep + step) & 7
+        push(bias_src.at[other & 3], bias_in.at[zh * 4 + rep], BIAS1, device(xy, other >> 2, core), other & 3)
     leaving.append((bias_in.at[pl.ds(0, 7)], BIAS1))
     bias_in[zh * 4 + rep] = bias_src[rep]
 
@@ -190,7 +190,7 @@
     bias[x, y, core] = block.astype(BF16)
     for step in (4, 3, 5, 2, 6, 1, 7):
         block = bias.at[x, y, core]
-        push(block, block, BIAS_Y, device(x * 8 + (y + step) % 8, zh, core), rep, recv_by.at[y])
+        push(block, block, BIAS_Y, device(x * 8 + ((y + step) & 7), zh, core), rep, recv_by.at[y])
     bias_along_x(y)
 
     def row_logits(s):
@@ -201,8 +201,8 @@
         logits[s] = dot_nt(expand_heads(wide), keys[s]).reshape(2, 4, 8, 16, RES)
 
     def nearest(turn):
-        away = (turn + 1) // 2
-        return (y + jnp.where(turn % 2 == 1, away, 8 - away)) % 8
+        away = (turn + 1) >> 1
+        return (y + jnp.where((turn & 1) == 1, away, 8 - away)) & 7
 
     def row_softmax(y_, which):
         offset = bias[:, y_, which].astype(F32).reshape(64, RES)
@@ -227,29 +227,36 @@
 
     row_logits(0)
     for step in (1, 7, 2, 6, 3, 5, 4):
-        source = (y + step) % 8
+        source = (y + step) & 7
         landed(bias.at[0, 0, 0], recv_by.at[source])
         bias_along_x(source)
     row_logits(1)
-
-    def own_queries(turn, _):
+    loaded(12)
+    final_t[...] = w_fin[...].astype(F32).T.astype(BF16)
+
+    def own_arrived(turn):
         source = nearest(turn)
         for other in range(1, 4):
-            landed(bias.at[0, 0, 0], recv_bx.at[((x + other) % 4) * 8 + source])
+            landed(bias.at[0, 0, 0], recv_bx.at[((x + other) & 3) * 8 + source])
         bias_to_core(source)
-        row_softmax(source, core)
-        return 0
-
-    def other_queries(turn, _):
+        return source
+
+    def other_arrived(turn):
         source = nearest(turn)
         landed(bias.at[:, 0, 0], recv_bc.at[source])
-        row_softmax(source, 1 - core)
+        return source
+
+    def both_queries(turn, _):
+        mine_, theirs = own_arrived(turn), other_arrived(turn - 1)
+        row_softmax(mine_, core)
+        row_softmax(theirs, 1 - core)
         return 0
 
     loaded(6)
-    lax.fori_loop(0, 8, own_queries, 0)
+    row_softmax(own_arrived(0), core)
+    lax.fori_loop(1, 8, both_queries, 0)
+    row_softmax(other_arrived(7), 1 - core)
     row_finish(core)
-    lax.fori_loop(0, 8, other_queries, 0)
     row_finish(1 - core)
     leaving.append((bias.at[0, pl.ds(0, 7), 0], BIAS_Y))
     leaving.append((bias.at[pl.ds(0, 3), :, 0], BIAS_X))
@@ -275,13 +282,13 @@
         ]
         col_src[target] = jnp.concatenate(parts, axis=0).astype(BF16)
     for step in range(1, 4):
-        other = (zc + step) % 4
-        push(col_src.at[other], col_in.at[zc], MSA2, device(xy, other // 2, other % 2), rep)
+        other = (zc + step) & 3
+        push(col_src.at[other], col_in.at[zc], MSA2, device(xy, other >> 1, other & 1), rep)
     leaving.append((col_in.at[pl.ds(0, 3)], MSA2))
     col_in[zc] = col_src[zc]
     arrived(col_in.at[pl.ds(0, 3)], MSA2)
 
-    loaded(7, 8, 9, 10, 11, 12)
+    loaded(7, 8, 9, 10, 11)
     middle = col_in[...].astype(F32).reshape(ROWS, FEAT)
     tokens = layer_norm(middle, g_col[...])
     projected = dot(tokens, w_col[...])
@@ -301,7 +308,7 @@
         col_denom[rows, :] = jnp.broadcast_to(1.0 / total, (128, 128))
         return 0
 
-    lax.fori_loop(0, 16, col_softmax, 0)
+    lax.fori_loop(0, 16, col_softmax, 0, unroll=2)
     attended = dot(col_weights[...], col_values)
     merged = merge_heads(attended, col_denom[...][:, :1])
     gated = (merged * col_gates).astype(BF16)
@@ -322,7 +329,7 @@
         right[y, zh] = right_src[...]
 
     for step in range(1, 4):
-        push(left_src, left.at[x, core, rep], LEFT, dap, (rep + step) % 4)
+        push(left_src, left.at[x, core, rep], LEFT, dap, (rep + step) & 3)
     leaving.append((None, RIGHT1))
     leaving.append((left.at[0, 0, pl.ds(0, 3)], LEFT))
     left[x, core, rep] = left_src[...]
@@ -337,7 +344,7 @@
     def right_along_y(zh_):
         for step in (4, 3, 5, 2, 6, 1, 7):
             block = right.at[y, zh_]
-            push(block, block, RIGHT_Y, device(x * 8 + (y + step) % 8, zh, core), rep)
+            push(block, block, RIGHT_Y, device(x * 8 + ((y + step) & 7), zh, core), rep, recv_ry.at[y])
 
     @pl.when(x != rep)
     def _():
@@ -347,13 +354,13 @@
     arrived(left.at[0, 0, pl.ds(0, 3)], LEFT)
     for step in (2, 1, 3):
         block = left.at[x, core]
-        push(block, block, LEFT_X, device(((x + step) % 4) * 8 + y, zh, core), rep)
+        push(block, block, LEFT_X, device(((x + step) & 3) * 8 + y, zh, core), rep)
     leaving.append((left.at[pl.ds(0, 3), 0], LEFT_X))
     landed(right_src, recv_r1.at[1 - zh])
     right_along_y(1 - zh)
     leaving.append((right.at[pl.ds(0, 7)], RIGHT_Y))
     for step in range(1, 4):
-        push(final.at[rep], final.at[rep], FINAL, dap, (rep + step) % 4)
+        push(final.at[rep], final.at[rep], FINAL, dap, (rep + step) & 3)
     leaving.append((final.at[pl.ds(0, 3)], FINAL))
     arrived(left.at[pl.ds(0, 3), 0], LEFT_X)
     block = left.at[:, core]
@@ -367,37 +374,38 @@
         left_t[pl.ds(channel * 32, 32), :] = jnp.concatenate(
             [left_f[half, pl.ds(channel, 32, stride=FACTOR), :] for half in range(2)], axis=1
         ).astype(BF16)
-    arrived(right.at[pl.ds(0, 7)], RIGHT_Y)
     quarter = lax.broadcasted_iota(jnp.int32, (FACTOR, 128), 1) // 32
-    right_all = right[...].reshape(16 * FACTOR, ROWS)
-    for part in range(4):
-        product = dot_nt(right_all, left_t[pl.ds(part * 256, 256), :])
-        for tile in range(2):
-            lanes = slice(tile * 128, (tile + 1) * 128)
-            for four in range(4):
-                blocks = [product[(four * 4 + jq) * FACTOR : (four * 4 + jq + 1) * FACTOR, lanes] for jq in range(4)]
-                for cq in range(4):
-                    moved = [
-                        blocks[jq] if jq == cq else pltpu.roll(blocks[jq], (32 * (jq - cq)) % 128, 1) for jq in range(4)
-                    ]
-                    joined = jnp.where(
-                        quarter < 2,
-                        jnp.where(quarter == 0, moved[0], moved[1]),
-                        jnp.where(quarter == 2, moved[2], moved[3]),
-                    )
-                    channel = part * 8 + tile * 4 + cq
-                    outer[pl.ds(channel * FACTOR, FACTOR), four * 128 : (four + 1) * 128] = joined.astype(BF16)
-    flat = lax.dot_general(w_fin[...], outer[...], (((0,), (0,)), ((), ())), preferred_element_type=F32)
     for four in range(4):
-        update[pl.ds(four * 128, 128), :] = flat[:, four * 128 : (four + 1) * 128].T
+        sources = (nearest(2 * four), nearest(2 * four + 1))
+        for source in sources if four else sources[1:]:
+            landed(right.at[0], recv_ry.at[source])
+        operand = jnp.concatenate([right[source].reshape(2 * FACTOR, ROWS) for source in sources], axis=0)
+        product = dot_nt(operand, left_t[...])
+        for tile in range(8):
+            blocks = [
+                product[jq * FACTOR : (jq + 1) * FACTOR, tile * 128 : (tile + 1) * 128] for jq in range(4)
+            ]
+            for cq in range(4):
+                moved = [
+                    blocks[jq] if jq == cq else pltpu.roll(blocks[jq], (32 * (jq - cq)) % 128, 1) for jq in range(4)
+                ]
+                joined = jnp.where(
+                    quarter < 2,
+                    jnp.where(quarter == 0, moved[0], moved[1]),
+                    jnp.where(quarter == 2, moved[2], moved[3]),
+                )
+                outer[pl.ds((tile * 4 + cq) * FACTOR, FACTOR), :] = joined.astype(BF16)
+        change = dot(final_t[...], outer[...]).T
+        for half, source in enumerate(sources):
+            update[pl.ds(pl.multiple_of(source * 64, 64), 64), :] = change[half * 64 : (half + 1) * 64]
 
     for target in range(8):
         for r_ in range(4):
             result_src[target, r_] = update[pl.ds(target * 4 + r_, 16, stride=32), :].astype(BF16)
     mine = x * 2 + core
     for step in range(1, 8):
-        other = (mine + step) % 8
-        push(result_src.at[other], result_in.at[mine], RESULT, device((other // 2) * 8 + y, zh, other % 2), rep)
+        other = (mine + step) & 7
+        push(result_src.at[other], result_in.at[mine], RESULT, device((other >> 1) * 8 + y, zh, other & 1), rep)
     leaving.append((result_in.at[pl.ds(0, 7)], RESULT))
     result_in[mine] = result_src[mine]
 
@@ -413,6 +421,19 @@
             out_pair[a, here, :] = pair[a, here, :] + result_in[source, a].astype(F32)
 
     finish()
+
+
+def hand_over(msa, pair, out_msa, out_pair, done):
+    part = ROWS * 2
+    copies = [
+        pltpu.make_async_copy(msa.at[pl.ds(k * part, part)], out_msa.at[pl.ds(k * part, part)], done.at[k])
+        for k in range(4)
+    ]
+    copies.append(pltpu.make_async_copy(pair, out_pair, done.at[4]))
+    for copy in copies:
+        copy.start()
+    for copy in copies:
+        copy.wait()
 
 
 def shards(
@@ -474,7 +495,8 @@
         pltpu.VMEM((8, 2, FACTOR, ROWS), BF16),
         pltpu.VMEM((2, 32 * FACTOR, 128), F32),
         pltpu.VMEM((32 * FACTOR, ROWS), BF16),
-        pltpu.VMEM((FACTOR * FACTOR, 512), BF16),
+        pltpu.VMEM((CZ, FACTOR * FACTOR), BF16),
+        pltpu.VMEM((FACTOR * FACTOR, 128), BF16),
         pltpu.VMEM((512, CZ), F32),
         pltpu.VMEM((8, 4, 16, CZ), BF16),
         pltpu.VMEM((8, 4, 16, CZ), BF16),
@@ -486,6 +508,7 @@
         pltpu.SemaphoreType.DMA((32,)),
         pltpu.SemaphoreType.DMA((8,)),
         pltpu.SemaphoreType.DMA((2,)),
+        pltpu.SemaphoreType.DMA((8,)),
     ]
     out_msa, out_pair = pl.pallas_call(
         kernel,
@@ -500,6 +523,18 @@
             collective_id=0, has_side_effects=True, vmem_limit_bytes=60 * 1024 * 1024
         ),
     )(*operands)
+    anywhere = pl.BlockSpec(memory_space=pl.ANY)
+    out_msa, out_pair = pl.pallas_call(
+        hand_over,
+        out_shape=(
+            jax.ShapeDtypeStruct((ROWS * 8, 128), F32),
+            jax.ShapeDtypeStruct((4, 128, CZ), F32),
+        ),
+        in_specs=[anywhere] * 2,
+        out_specs=(anywhere, anywhere),
+        scratch_shapes=[pltpu.SemaphoreType.DMA((5,))],
+        compiler_params=pltpu.CompilerParams(vmem_limit_bytes=60 * 1024 * 1024),
+    )(out_msa, out_pair)
     return jnp.swapaxes(out_msa.reshape(ROWS, 2, 4, 128), 1, 2).reshape(ROWS, 4, FEAT), out_pair
 
 

time: 76.5 us -> 115 us (1.50)
  Pallas kernels: 72.6 us -> 114 us
  local copies, waits for them, and re-layouts: 3.12 us -> 0 us
    pallas_call x0 -> x1, Pallas kernels: none -> 40.9 us  [shards(): pl.pallas_call(hand_over, out_shape=(jax.ShapeDtypeStruct((ROWS * 8, 128)...]
    unnamed x4 -> x0, local copies, waits for them, and re-layouts: 3.12 us -> none
where the time goes in v5:
time: 115 us; the launch traced here: 114 us
  Pallas kernels  114 us (99%)
    pallas_call x1, Pallas kernels, shards(): pl.pallas_call(kernel, out_shape=(jax.ShapeDtypeStruct((ROWS * 8, 128), F...  72.9 us
    pallas_call x1, Pallas kernels, shards(): pl.pallas_call(hand_over, out_shape=(jax.ShapeDtypeStruct((ROWS * 8, 128)...  40.9 us

profile of v5, /device:TPU:1, one launch (start us, length us, event | category | flops | bytes accessed | tf_op | source)
XLA Modules:
  0.0 114.4 jit_solution(4999275030906722977)
XLA Ops:
  0.6 72.9 %shard_map.140 = (f32[2048,128]{1,0:T(8,128)}, f32[4,128,128]{2,1,0:T(8,128)}) custom-call(f32[2,512,256]{2,1,0:T(8,128)} %refs_0_.1, f32[4,128,128]{2,1,0:T(8,128)} %refs_1_.1, f32[1,256]{1,0:T(1,128)} %bitcast.13, bf16[256,1024]{1,0:T(8,128)(2,1)} %refs_3_.1, f32[1,128]{1,0:T(1,128)} %bitcast.16, bf16[8,128]{1,0:T(8,128)(2,1)} %bitcast.12, ...), custom_call_target="tpu_custom_call" | custom-call | tf_op jit(solution)/shard_map/pallas_call | solution.py:513
  73.5 40.9 %shard_map.141 = (f32[2048,128]{1,0:T(8,128)}, f32[4,128,128]{2,1,0:T(8,128)}) custom-call(f32[2048,128]{1,0:T(8,128)} %get-tuple-element.6.msa, f32[4,128,128]{2,1,0:T(8,128)} %get-tuple-element.7.pair), custom_call_target="tpu_custom_call" | custom-call | tf_op jit(solution)/shard_map/pallas_call | solution.py:527

commit v6 on v5

--- a/solution.py
+++ b/solution.py
@@ -64,7 +64,7 @@
         bias_src, bias_in, bias, queries, gates, keys, values, logits, weights, denom, staged, msa_src, msa_in,
         unpacked, col_src, col_in, col_logits, col_weights, col_denom, natural, final, left_src, left, right_src, right,
         left_f, left_t, final_t, outer, update, result_src, result_in, msa_halves,
-        send, recv, load, recv_by, recv_bx, recv_bc, recv_r1, recv_ry,
+        send, recv, load, recv_by, recv_bx, recv_bc, recv_r1, recv_ry, recv_lx, recv_lc,
     ) = rest
     loads = [pltpu.make_async_copy(given[k], held[k], load.at[k]) for k in range(13)]
     for k in (1, 5, 4):
@@ -346,30 +346,46 @@
             block = right.at[y, zh_]
             push(block, block, RIGHT_Y, device(x * 8 + ((y + step) & 7), zh, core), rep, recv_ry.at[y])
 
+    def left_to_core(x_):
+        block = left.at[x_, core]
+        push(block, block, LEFT_C, device(xy, zh, 1 - core), rep, recv_lc.at[x_])
+
+    def left_unpack(x_, core_):
+        rows = pl.ds(pl.multiple_of((x_ * 2 + core_) * 128, 128), 128)
+        block = left[x_, core_].astype(F32).reshape(128, ROWS)
+        for half in range(2):
+            left_f[half, rows, :] = block[:, half * 128 : (half + 1) * 128]
+
+    arrived(left.at[0, 0, pl.ds(0, 3)], LEFT)
+    for step in (2, 1, 3):
+        block = left.at[x, core]
+        push(block, block, LEFT_X, device(((x + step) & 3) * 8 + y, zh, core), rep, recv_lx.at[x])
+    left_to_core(x)
+
     @pl.when(x != rep)
     def _():
         landed(right_src, recv_r1.at[zh])
 
     right_along_y(zh)
-    arrived(left.at[0, 0, pl.ds(0, 3)], LEFT)
-    for step in (2, 1, 3):
-        block = left.at[x, core]
-        push(block, block, LEFT_X, device(((x + step) & 3) * 8 + y, zh, core), rep)
-    leaving.append((left.at[pl.ds(0, 3), 0], LEFT_X))
     landed(right_src, recv_r1.at[1 - zh])
     right_along_y(1 - zh)
     leaving.append((right.at[pl.ds(0, 7)], RIGHT_Y))
     for step in range(1, 4):
         push(final.at[rep], final.at[rep], FINAL, dap, (rep + step) & 3)
     leaving.append((final.at[pl.ds(0, 3)], FINAL))
-    arrived(left.at[pl.ds(0, 3), 0], LEFT_X)
-    block = left.at[:, core]
-    push(block, block, LEFT_C, device(xy, zh, 1 - core), rep)
+    left_unpack(x, core)
+    for step in (1, 3, 2):
+        source = (x + step) & 3
+        landed(left.at[0, 0], recv_lx.at[source])
+        left_to_core(source)
+        left_unpack(source, core)
+    leaving.append((left.at[pl.ds(0, 3), 0], LEFT_X))
     leaving.append((left.at[:, 0], LEFT_C))
-    arrived(left.at[:, 0], LEFT_C)
-
-    for half in range(2):
-        left_f[half] = left[..., half * 128 : (half + 1) * 128].astype(F32).reshape(32 * FACTOR, 128)
+    for step in (0, 1, 3, 2):
+        source = (x + step) & 3
+        landed(left.at[0, 0], recv_lc.at[source])
+        left_unpack(source, 1 - core)
+
     for channel in range(FACTOR):
         left_t[pl.ds(channel * 32, 32), :] = jnp.concatenate(
             [left_f[half, pl.ds(channel, 32, stride=FACTOR), :] for half in range(2)], axis=1
@@ -421,19 +437,6 @@
             out_pair[a, here, :] = pair[a, here, :] + result_in[source, a].astype(F32)
 
     finish()
-
-
-def hand_over(msa, pair, out_msa, out_pair, done):
-    part = ROWS * 2
-    copies = [
-        pltpu.make_async_copy(msa.at[pl.ds(k * part, part)], out_msa.at[pl.ds(k * part, part)], done.at[k])
-        for k in range(4)
-    ]
-    copies.append(pltpu.make_async_copy(pair, out_pair, done.at[4]))
-    for copy in copies:
-        copy.start()
-    for copy in copies:
-        copy.wait()
 
 
 def shards(
@@ -509,6 +512,8 @@
         pltpu.SemaphoreType.DMA((8,)),
         pltpu.SemaphoreType.DMA((2,)),
         pltpu.SemaphoreType.DMA((8,)),
+        pltpu.SemaphoreType.DMA((4,)),
+        pltpu.SemaphoreType.DMA((4,)),
     ]
     out_msa, out_pair = pl.pallas_call(
         kernel,
@@ -520,21 +525,9 @@
         out_specs=(vmem, vmem),
         scratch_shapes=scratch,
         compiler_params=pltpu.CompilerParams(
-            collective_id=0, has_side_effects=True, vmem_limit_bytes=60 * 1024 * 1024
+            collective_id=0, has_side_effects=True, vmem_limit_bytes=44 * 1024 * 1024
         ),
-    )(*operands)
-    anywhere = pl.BlockSpec(memory_space=pl.ANY)
-    out_msa, out_pair = pl.pallas_call(
-        hand_over,
-        out_shape=(
-            jax.ShapeDtypeStruct((ROWS * 8, 128), F32),
-            jax.ShapeDtypeStruct((4, 128, CZ), F32),
-        ),
-        in_specs=[anywhere] * 2,
-        out_specs=(anywhere, anywhere),
-        scratch_shapes=[pltpu.SemaphoreType.DMA((5,))],
-        compiler_params=pltpu.CompilerParams(vmem_limit_bytes=60 * 1024 * 1024),
-    )(out_msa, out_pair)
+    )(*[pltpu.with_memory_space_constraint(a, pltpu.HBM) for a in operands])
     return jnp.swapaxes(out_msa.reshape(ROWS, 2, 4, 128), 1, 2).reshape(ROWS, 4, FEAT), out_pair
 
 

time: 115 us -> 74.3 us (0.65)
  Pallas kernels: 114 us -> 71.8 us
  local copies, waits for them, and re-layouts: 0 us -> 1.67 us
    pallas_call x1 -> x0, Pallas kernels: 40.9 us -> none  [shards(): pl.pallas_call(hand_over, out_shape=(jax.ShapeDtypeStruct((ROWS * 8, 128)...]
    unnamed x0 -> x2, local copies, waits for them, and re-layouts: none -> 1.67 us
where the time goes in v6:
time: 74.3 us; the launch traced here: 74.2 us
  Pallas kernels  71.8 us (97%)
  local copies, waits for them, and re-layouts  1.67 us (2%)
    pallas_call x1, Pallas kernels, shards(): pl.pallas_call(kernel, out_shape=(jax.ShapeDtypeStruct((ROWS * 8, 128), F...  71.8 us
    unnamed x2, local copies, waits for them, and re-layouts  1.67 us

profile of v6, /device:TPU:1, one launch (start us, length us, event | category | flops | bytes accessed | tf_op | source)
XLA Modules:
  0.0 74.2 jit_solution(6655632174688723440)
XLA Ops:
  0.6 71.8 %shard_map.140 = (f32[2048,128]{1,0:T(8,128)S(1)}, f32[4,128,128]{2,1,0:T(8,128)S(1)}) custom-call(f32[2,512,256]{2,1,0:T(8,128)} %refs_0_.1, f32[4,128,128]{2,1,0:T(8,128)} %refs_1_.1, f32[1,256]{1,0:T(1,128)} %bitcast.14, bf16[256,1024]{1,0:T(8,128)(2,1)} %refs_3_.1, f32[1,128]{1,0:T(1,128)} %bitcast.17, bf16[8,128]{1,0:T(8,128)(2,1)} %bitcast.13, ...), custom_call_target="tpu_custom_call" | custom-call | tf_op jit(solution)/shard_map/pallas_call | solution.py:518
  72.5 1.0 %copy.18 = f32[256,4,256]{2,1,0:T(4,128)} copy(f32[256,4,256]{2,1,0:T(4,128)S(1)} %bitcast.11) | data formatting | bytes 2097152
  73.5 0.7 copy.19

commit v7 on v6

--- a/solution.py
+++ b/solution.py
@@ -64,7 +64,7 @@
         bias_src, bias_in, bias, queries, gates, keys, values, logits, weights, denom, staged, msa_src, msa_in,
         unpacked, col_src, col_in, col_logits, col_weights, col_denom, natural, final, left_src, left, right_src, right,
         left_f, left_t, final_t, outer, update, result_src, result_in, msa_halves,
-        send, recv, load, recv_by, recv_bx, recv_bc, recv_r1, recv_ry, recv_lx, recv_lc,
+        send, recv, load, recv_by, recv_bx, recv_bc, recv_r1, recv_ry, recv_lx, recv_lc, recv_m1,
     ) = rest
     loads = [pltpu.make_async_copy(given[k], held[k], load.at[k]) for k in range(13)]
     for k in (1, 5, 4):
@@ -265,27 +265,30 @@
 
     def push_msa(turn, _):
         other = far_first(turn)
-        push(msa_src.at[other], msa_in.at[xy], MSA1, device(other, zh, core), rep)
+        push(msa_src.at[other], msa_in.at[xy], MSA1, device(other, zh, core), rep, recv_m1.at[x])
         return 0
 
     lax.fori_loop(0, 31, push_msa, 0)
     leaving.append((msa_in.at[pl.ds(0, 31)], MSA1))
     msa_in[xy] = msa_src[xy]
-    arrived(msa_in.at[pl.ds(0, 31)], MSA1)
-    unpacked[...] = msa_in[...].astype(F32).reshape(512, 128)
-    for target in range(4):
-        parts = [
-            jnp.concatenate(
-                [unpacked[pl.ds(target * 4 + s * 2 + half, 32, stride=16), :] for half in range(2)], axis=1
-            )
-            for s in range(2)
-        ]
-        col_src[target] = jnp.concatenate(parts, axis=0).astype(BF16)
-    for step in range(1, 4):
-        other = (zc + step) & 3
-        push(col_src.at[other], col_in.at[zc], MSA2, device(xy, other >> 1, other & 1), rep)
+    for step in (0, 1, 3, 2):
+        source = (x + step) & 3
+        landed(msa_in.at[pl.ds(0, 8 if step else 7)], recv_m1.at[source])
+        start = pl.multiple_of(source * 128, 128)
+        unpacked[pl.ds(start, 128), :] = msa_in[pl.ds(source * 8, 8)].astype(F32).reshape(128, 128)
+        for target in range(4):
+            parts = [
+                jnp.concatenate(
+                    [unpacked[pl.ds(start + target * 4 + s * 2 + half, 8, stride=16), :] for half in range(2)], axis=1
+                )
+                for s in range(2)
+            ]
+            col_src[target, source] = jnp.concatenate(parts, axis=0).astype(BF16)
+        for turn in range(1, 4):
+            other = (zc + turn) & 3
+            push(col_src.at[other, source], col_in.at[zc, source], MSA2, device(xy, other >> 1, other & 1), rep)
+        col_in[zc, source] = col_src[zc, source]
     leaving.append((col_in.at[pl.ds(0, 3)], MSA2))
-    col_in[zc] = col_src[zc]
     arrived(col_in.at[pl.ds(0, 3)], MSA2)
 
     loaded(7, 8, 9, 10, 11)
@@ -318,6 +321,8 @@
     factors = dot_nt(w_fac[...], ln_opm)
     right_src[...] = factors[FACTOR:].astype(BF16)
     left_src[...] = (factors[:FACTOR] * (1.0 / ROWS)).astype(BF16)
+    for step in range(1, 4):
+        push(left_src, left.at[x, core, rep], LEFT, dap, (rep + step) & 3)
     push(right_src, right.at[y, zh], RIGHT1, device(mirror, 1 - zh, core), x, recv_r1.at[zh])
 
     @pl.when(x != rep)
@@ -328,18 +333,15 @@
     def _():
         right[y, zh] = right_src[...]
 
-    for step in range(1, 4):
-        push(left_src, left.at[x, core, rep], LEFT, dap, (rep + step) & 3)
     leaving.append((None, RIGHT1))
     leaving.append((left.at[0, 0, pl.ds(0, 3)], LEFT))
     left[x, core, rep] = left_src[...]
-    for m_ in range(4):
-        for s in range(2):
-            start = (m_ * 2 + s) * 32
-            for half in range(2):
-                natural[half, pl.ds(m_ * 2 + s, 32, stride=8), :] = target_rows[
-                    start : start + 32, half * 128 : (half + 1) * 128
-                ]
+    for block in range(32):
+        m_, x_, s = block // 8, (block // 2) % 4, block % 2
+        for half in range(2):
+            natural[half, pl.ds(x_ * 64 + m_ * 2 + s, 8, stride=8), :] = target_rows[
+                block * 8 : (block + 1) * 8, half * 128 : (half + 1) * 128
+            ]
     final[rep] = jnp.concatenate([natural[0], natural[1]], axis=1).astype(BF16)
     def right_along_y(zh_):
         for step in (4, 3, 5, 2, 6, 1, 7):
@@ -391,29 +393,29 @@
             [left_f[half, pl.ds(channel, 32, stride=FACTOR), :] for half in range(2)], axis=1
         ).astype(BF16)
     quarter = lax.broadcasted_iota(jnp.int32, (FACTOR, 128), 1) // 32
+    for turn in range(1, 8):
+        landed(right.at[0], recv_ry.at[nearest(turn)])
+    right_all = right[...].reshape(16 * FACTOR, ROWS)
+    for part in range(4):
+        product = dot_nt(right_all, left_t[pl.ds(part * 256, 256), :])
+        for tile in range(2):
+            lanes = slice(tile * 128, (tile + 1) * 128)
+            for four in range(4):
+                blocks = [product[(four * 4 + jq) * FACTOR : (four * 4 + jq + 1) * FACTOR, lanes] for jq in range(4)]
+                for cq in range(4):
+                    moved = [
+                        blocks[jq] if jq == cq else pltpu.roll(blocks[jq], (32 * (jq - cq)) % 128, 1) for jq in range(4)
+                    ]
+                    joined = jnp.where(
+                        quarter < 2,
+                        jnp.where(quarter == 0, moved[0], moved[1]),
+                        jnp.where(quarter == 2, moved[2], moved[3]),
+                    )
+                    channel = part * 8 + tile * 4 + cq
+                    outer[pl.ds(channel * FACTOR, FACTOR), four * 128 : (four + 1) * 128] = joined.astype(BF16)
+    flat = dot(final_t[...], outer[...])
     for four in range(4):
-        sources = (nearest(2 * four), nearest(2 * four + 1))
-        for source in sources if four else sources[1:]:
-            landed(right.at[0], recv_ry.at[source])
-        operand = jnp.concatenate([right[source].reshape(2 * FACTOR, ROWS) for source in sources], axis=0)
-        product = dot_nt(operand, left_t[...])
-        for tile in range(8):
-            blocks = [
-                product[jq * FACTOR : (jq + 1) * FACTOR, tile * 128 : (tile + 1) * 128] for jq in range(4)
-            ]
-            for cq in range(4):
-                moved = [
-                    blocks[jq] if jq == cq else pltpu.roll(blocks[jq], (32 * (jq - cq)) % 128, 1) for jq in range(4)
-                ]
-                joined = jnp.where(
-                    quarter < 2,
-                    jnp.where(quarter == 0, moved[0], moved[1]),
-                    jnp.where(quarter == 2, moved[2], moved[3]),
-                )
-                outer[pl.ds((tile * 4 + cq) * FACTOR, FACTOR), :] = joined.astype(BF16)
-        change = dot(final_t[...], outer[...]).T
-        for half, source in enumerate(sources):
-            update[pl.ds(pl.multiple_of(source * 64, 64), 64), :] = change[half * 64 : (half + 1) * 64]
+        update[pl.ds(four * 128, 128), :] = flat[:, four * 128 : (four + 1) * 128].T
 
     for target in range(8):
         for r_ in range(4):
@@ -485,8 +487,8 @@
         pltpu.VMEM((32, 16, 128), BF16),
         pltpu.VMEM((32, 16, 128), BF16),
         pltpu.VMEM((512, 128), F32),
-        pltpu.VMEM((4, 64, FEAT), BF16),
-        pltpu.VMEM((4, 64, FEAT), BF16),
+        pltpu.VMEM((4, 4, 16, FEAT), BF16),
+        pltpu.VMEM((4, 4, 16, FEAT), BF16),
         pltpu.VMEM((ROWS * HEADS, ROWS), F32),
         pltpu.VMEM((ROWS * HEADS, ROWS), BF16),
         pltpu.VMEM((ROWS * HEADS, 128), F32),
@@ -499,7 +501,7 @@
         pltpu.VMEM((2, 32 * FACTOR, 128), F32),
         pltpu.VMEM((32 * FACTOR, ROWS), BF16),
         pltpu.VMEM((CZ, FACTOR * FACTOR), BF16),
-        pltpu.VMEM((FACTOR * FACTOR, 128), BF16),
+        pltpu.VMEM((FACTOR * FACTOR, 512), BF16),
         pltpu.VMEM((512, CZ), F32),
         pltpu.VMEM((8, 4, 16, CZ), BF16),
         pltpu.VMEM((8, 4, 16, CZ), BF16),
@@ -512,6 +514,7 @@
         pltpu.SemaphoreType.DMA((8,)),
         pltpu.SemaphoreType.DMA((2,)),
         pltpu.SemaphoreType.DMA((8,)),
+        pltpu.SemaphoreType.DMA((4,)),
         pltpu.SemaphoreType.DMA((4,)),
         pltpu.SemaphoreType.DMA((4,)),
     ]

time: 74.3 us -> 73.9 us (level)
  no operation moved by 1% of the time
where the time goes in v7:
time: 73.9 us; the launch traced here: 73.8 us
  Pallas kernels  71.5 us (97%)
  local copies, waits for them, and re-layouts  1.67 us (2%)
    pallas_call x1, Pallas kernels, shards(): pl.pallas_call(kernel, out_shape=(jax.ShapeDtypeStruct((ROWS * 8, 128), F...  71.5 us
    unnamed x2, local copies, waits for them, and re-layouts  1.67 us

profile of v7, /device:TPU:1, one launch (start us, length us, event | category | flops | bytes accessed | tf_op | source)
XLA Modules:
  0.0 73.8 jit_solution(12796889272564110848)
XLA Ops:
  0.6 71.5 %shard_map.140 = (f32[2048,128]{1,0:T(8,128)S(1)}, f32[4,128,128]{2,1,0:T(8,128)S(1)}) custom-call(f32[2,512,256]{2,1,0:T(8,128)} %refs_0_.1, f32[4,128,128]{2,1,0:T(8,128)} %refs_1_.1, f32[1,256]{1,0:T(1,128)} %bitcast.14, bf16[256,1024]{1,0:T(8,128)(2,1)} %refs_3_.1, f32[1,128]{1,0:T(1,128)} %bitcast.17, bf16[8,128]{1,0:T(8,128)(2,1)} %bitcast.13, ...), custom_call_target="tpu_custom_call" | custom-call | tf_op jit(solution)/shard_map/pallas_call | solution.py:521
  72.1 1.0 %copy.18 = f32[256,4,256]{2,1,0:T(4,128)} copy(f32[256,4,256]{2,1,0:T(4,128)S(1)} %bitcast.11) | data formatting | bytes 2097152
  73.1 0.7 copy.19

commit v8 on v7

--- a/solution.py
+++ b/solution.py
@@ -22,6 +22,7 @@
 
 BIAS1, BIAS_Y, BIAS_X, BIAS_C, MSA1, MSA2, LEFT, LEFT_X, LEFT_C, FINAL, RIGHT1, RIGHT_Y, RESULT = range(13)
 PHASES = 13
+SHEET_STEPS = (10, 8, 9, 11, 6, 7, 5, 14, 13, 15, 2, 3, 1, 12, 4)
 
 
 def layer_norm(values, gain):
@@ -64,7 +65,7 @@
         bias_src, bias_in, bias, queries, gates, keys, values, logits, weights, denom, staged, msa_src, msa_in,
         unpacked, col_src, col_in, col_logits, col_weights, col_denom, natural, final, left_src, left, right_src, right,
         left_f, left_t, final_t, outer, update, result_src, result_in, msa_halves,
-        send, recv, load, recv_by, recv_bx, recv_bc, recv_r1, recv_ry, recv_lx, recv_lc, recv_m1,
+        send, recv, load, recv_by, recv_bx, recv_bc, recv_r1, recv_ry, recv_lx, recv_lc,
     ) = rest
     loads = [pltpu.make_async_copy(given[k], held[k], load.at[k]) for k in range(13)]
     for k in (1, 5, 4):
@@ -91,13 +92,6 @@
     def greet(dap_, rep_):
         pl.semaphore_signal(barrier, inc=1, device_id=(dap_, rep_), device_id_type=MESH)
 
-    def far_first(turn):
-        return (xy + turn + jnp.where(turn < 20, 12, -19)) & 31
-
-    def greet_xy(turn, _):
-        greet(device(far_first(turn), zh, core), rep)
-        return 0
-
     mirror = rep * 8 + y
     greet(device(mirror, 1 - zh, core), x)
 
@@ -105,13 +99,18 @@
     def _():
         greet(device(mirror, zh, core), x)
 
-    lax.fori_loop(0, 31, greet_xy, 0)
+    place = x * 4 + zc
+
+    def sheet(other):
+        return device((other >> 2) * 8 + y, (other >> 1) & 1, other & 1)
+
+    for step in SHEET_STEPS:
+        greet(sheet((place + step) & 15), rep)
     for step in (4, 3, 5, 2, 6, 1, 7):
         other = (zh * 4 + rep + step) & 7
         greet(device(xy, other >> 2, core), other & 3)
-    for step in range(4):
-        greet(device(((x + step) & 3) * 8 + y, zh, 1 - core), rep)
-    greet(device(xy, 1 - zh, 1 - core), rep)
+    for step in (4, 3, 5, 2, 6, 1, 7):
+        greet(device(x * 8 + ((y + step) & 7), zh, core), rep)
     for k in (0, 2, 3, 6, 12, 7, 8, 9, 10, 11):
         loads[k].start()
 
@@ -161,7 +160,7 @@
     for a in range(4):
         bias_src[a] = head_bias[:, a * 128 : (a + 1) * 128]
 
-    pl.semaphore_wait(barrier, 44 + jnp.where(x != rep, 1, 0))
+    pl.semaphore_wait(barrier, 30 + jnp.where(x != rep, 1, 0))
 
     for step in (4, 3, 5, 2, 6, 1, 7):
         other = (zh * 4 + rep + step) & 7
@@ -177,11 +176,12 @@
         values[s] = projected[:, FEAT:]
         for half in range(2):
             msa_halves[s, half] = msa[s, :, half * 128 : (half + 1) * 128]
-            for h_ in range(2):
-                for c_ in range(2):
-                    queries[s, c_, half, pl.ds(h_, 32, stride=2), :] = msa_halves[
-                        s, half, pl.ds(8 * h_ + 4 * c_ + rep, 32, stride=16), :
-                    ]
+            for x_ in range(4):
+                for h_ in range(2):
+                    for c_ in range(2):
+                        queries[s, c_, half, pl.ds(x_ * 2 + h_, 8, stride=8), :] = msa_halves[
+                            s, half, pl.ds(128 * x_ + 8 * h_ + 4 * c_ + rep, 8, stride=16), :
+                        ]
 
     arrived(bias_in.at[pl.ds(0, 7)], BIAS1)
     block = jnp.concatenate(
@@ -198,7 +198,7 @@
         tokens = layer_norm(jnp.concatenate(halves, axis=1), g_row[...])
         wide = dot(tokens, w_row[:, :FEAT]) * LOGIT_SCALE
         gates[s] = jax.nn.sigmoid(dot(tokens, w_row[:, 3 * FEAT :])).reshape(2, 64, FEAT)
-        logits[s] = dot_nt(expand_heads(wide), keys[s]).reshape(2, 4, 8, 16, RES)
+        logits[s] = dot_nt(expand_heads(wide), keys[s]).reshape(2, 8, 4, 16, RES)
 
     def nearest(turn):
         away = (turn + 1) >> 1
@@ -207,12 +207,12 @@
     def row_softmax(y_, which):
         offset = bias[:, y_, which].astype(F32).reshape(64, RES)
         for s in range(2):
-            raw = logits[s, which, :, y_].reshape(64, RES) + offset
+            raw = logits[s, which, y_].reshape(64, RES) + offset
             top = jnp.max(raw, axis=-1, keepdims=True)
             powers = jnp.exp2(raw - top)
             total = jnp.sum(powers, axis=-1, keepdims=True)
-            weights[s, which, :, y_] = powers.astype(BF16).reshape(4, 16, RES)
-            denom[s, which, :, y_] = jnp.broadcast_to(1.0 / total, (64, 128)).reshape(4, 16, 128)
+            weights[s, which, y_] = powers.astype(BF16).reshape(4, 16, RES)
+            denom[s, which, y_] = jnp.broadcast_to(1.0 / total, (64, 128)).reshape(4, 16, 128)
 
     def row_finish(which):
         for s in range(2):
@@ -261,35 +261,27 @@
     leaving.append((bias.at[0, pl.ds(0, 7), 0], BIAS_Y))
     leaving.append((bias.at[pl.ds(0, 3), :, 0], BIAS_X))
     leaving.append((bias.at[:, :, 0], BIAS_C))
-    msa_src[...] = staged[...].astype(BF16).reshape(32, 16, 128)
-
-    def push_msa(turn, _):
-        other = far_first(turn)
-        push(msa_src.at[other], msa_in.at[xy], MSA1, device(other, zh, core), rep, recv_m1.at[x])
-        return 0
-
-    lax.fori_loop(0, 31, push_msa, 0)
-    leaving.append((msa_in.at[pl.ds(0, 31)], MSA1))
-    msa_in[xy] = msa_src[xy]
-    for step in (0, 1, 3, 2):
-        source = (x + step) & 3
-        landed(msa_in.at[pl.ds(0, 8 if step else 7)], recv_m1.at[source])
-        start = pl.multiple_of(source * 128, 128)
-        unpacked[pl.ds(start, 128), :] = msa_in[pl.ds(source * 8, 8)].astype(F32).reshape(128, 128)
-        for target in range(4):
-            parts = [
-                jnp.concatenate(
-                    [unpacked[pl.ds(start + target * 4 + s * 2 + half, 8, stride=16), :] for half in range(2)], axis=1
-                )
-                for s in range(2)
-            ]
-            col_src[target, source] = jnp.concatenate(parts, axis=0).astype(BF16)
-        for turn in range(1, 4):
-            other = (zc + turn) & 3
-            push(col_src.at[other, source], col_in.at[zc, source], MSA2, device(xy, other >> 1, other & 1), rep)
-        col_in[zc, source] = col_src[zc, source]
-    leaving.append((col_in.at[pl.ds(0, 3)], MSA2))
-    arrived(col_in.at[pl.ds(0, 3)], MSA2)
+    msa_src[...] = staged[...].astype(BF16).reshape(8, 64, 128)
+
+    for step in (4, 3, 5, 2, 6, 1, 7):
+        other = (y + step) & 7
+        push(msa_src.at[other], msa_in.at[y], MSA1, device(x * 8 + other, zh, core), rep)
+    leaving.append((msa_in.at[pl.ds(0, 7)], MSA1))
+    msa_in[y] = msa_src[y]
+    arrived(msa_in.at[pl.ds(0, 7)], MSA1)
+    unpacked[...] = msa_in[...].astype(F32).reshape(512, 128)
+    for target in range(16):
+        parts = [
+            jnp.concatenate([unpacked[pl.ds(target * 4 + s * 2 + half, 8, stride=64), :] for half in range(2)], axis=1)
+            for s in range(2)
+        ]
+        col_src[target] = jnp.concatenate(parts, axis=0).astype(BF16)
+    for step in SHEET_STEPS:
+        other = (place + step) & 15
+        push(col_src.at[other], col_in.at[place], MSA2, sheet(other), rep)
+    leaving.append((col_in.at[pl.ds(0, 15)], MSA2))
+    col_in[place] = col_src[place]
+    arrived(col_in.at[pl.ds(0, 15)], MSA2)
 
     loaded(7, 8, 9, 10, 11)
     middle = col_in[...].astype(F32).reshape(ROWS, FEAT)
@@ -337,7 +329,7 @@
     leaving.append((left.at[0, 0, pl.ds(0, 3)], LEFT))
     left[x, core, rep] = left_src[...]
     for block in range(32):
-        m_, x_, s = block // 8, (block // 2) % 4, block % 2
+        x_, m_, s = block // 8, (block // 2) % 4, block % 2
         for half in range(2):
             natural[half, pl.ds(x_ * 64 + m_ * 2 + s, 8, stride=8), :] = target_rows[
                 block * 8 : (block + 1) * 8, half * 128 : (half + 1) * 128
@@ -480,15 +472,15 @@
         pltpu.VMEM((2, 2, 64, FEAT), F32),
         pltpu.VMEM((2, RES, FEAT), BF16),
         pltpu.VMEM((2, RES, FEAT), BF16),
-        pltpu.VMEM((2, 2, 4, 8, 16, RES), F32),
-        pltpu.VMEM((2, 2, 4, 8, 16, RES), BF16),
-        pltpu.VMEM((2, 2, 4, 8, 16, 128), F32),
+        pltpu.VMEM((2, 2, 8, 4, 16, RES), F32),
+        pltpu.VMEM((2, 2, 8, 4, 16, RES), BF16),
+        pltpu.VMEM((2, 2, 8, 4, 16, 128), F32),
         pltpu.VMEM((512, 128), F32),
-        pltpu.VMEM((32, 16, 128), BF16),
-        pltpu.VMEM((32, 16, 128), BF16),
+        pltpu.VMEM((8, 64, 128), BF16),
+        pltpu.VMEM((8, 64, 128), BF16),
         pltpu.VMEM((512, 128), F32),
-        pltpu.VMEM((4, 4, 16, FEAT), BF16),
-        pltpu.VMEM((4, 4, 16, FEAT), BF16),
+        pltpu.VMEM((16, 16, FEAT), BF16),
+        pltpu.VMEM((16, 16, FEAT), BF16),
         pltpu.VMEM((ROWS * HEADS, ROWS), F32),
         pltpu.VMEM((ROWS * HEADS, ROWS), BF16),
         pltpu.VMEM((ROWS * HEADS, 128), F32),
@@ -516,7 +508,6 @@
         pltpu.SemaphoreType.DMA((8,)),
         pltpu.SemaphoreType.DMA((4,)),
         pltpu.SemaphoreType.DMA((4,)),
-        pltpu.SemaphoreType.DMA((4,)),
     ]
     out_msa, out_pair = pl.pallas_call(
         kernel,

time: 73.9 us -> 76 us (1.028)
  Pallas kernels: 71.5 us -> 73.5 us
    pallas_call x1, Pallas kernels: 71.5 us -> 73.5 us  [shards(): pl.pallas_call(kernel, out_shape=(jax.ShapeDtypeStruct((ROWS * 8, 128), F...]
where the time goes in v8:
time: 76 us; the launch traced here: 75.8 us
  Pallas kernels  73.5 us (97%)
  local copies, waits for them, and re-layouts  1.67 us (2%)
    pallas_call x1, Pallas kernels, shards(): pl.pallas_call(kernel, out_shape=(jax.ShapeDtypeStruct((ROWS * 8, 128), F...  73.5 us
    unnamed x2, local copies, waits for them, and re-layouts  1.67 us

profile of v8, /device:TPU:1, one launch (start us, length us, event | category | flops | bytes accessed | tf_op | source)
XLA Modules:
  0.0 75.8 jit_solution(5176140165800584507)
XLA Ops:
  0.6 73.5 %shard_map.140 = (f32[2048,128]{1,0:T(8,128)S(1)}, f32[4,128,128]{2,1,0:T(8,128)S(1)}) custom-call(f32[2,512,256]{2,1,0:T(8,128)} %refs_0_.1, f32[4,128,128]{2,1,0:T(8,128)} %refs_1_.1, f32[1,256]{1,0:T(1,128)} %bitcast.14, bf16[256,1024]{1,0:T(8,128)(2,1)} %refs_3_.1, f32[1,128]{1,0:T(1,128)} %bitcast.17, bf16[8,128]{1,0:T(8,128)(2,1)} %bitcast.13, ...), custom_call_target="tpu_custom_call" | custom-call | tf_op jit(solution)/shard_map/pallas_call | solution.py:512
  74.2 1.0 %copy.18 = f32[256,4,256]{2,1,0:T(4,128)} copy(f32[256,4,256]{2,1,0:T(4,128)S(1)} %bitcast.11) | data formatting | bytes 2097152
  75.1 0.7 copy.19

commit v9 on v7

--- a/solution.py
+++ b/solution.py
@@ -311,7 +311,7 @@
         col_denom[rows, :] = jnp.broadcast_to(1.0 / total, (128, 128))
         return 0
 
-    lax.fori_loop(0, 16, col_softmax, 0, unroll=2)
+    lax.fori_loop(0, 16, col_softmax, 0, unroll=4)
     attended = dot(col_weights[...], col_values)
     merged = merge_heads(attended, col_denom[...][:, :1])
     gated = (merged * col_gates).astype(BF16)
@@ -417,15 +417,18 @@
     for four in range(4):
         update[pl.ds(four * 128, 128), :] = flat[:, four * 128 : (four + 1) * 128].T
 
-    for target in range(8):
+    mine = x * 2 + core
+
+    def result_of(target, into):
         for r_ in range(4):
-            result_src[target, r_] = update[pl.ds(target * 4 + r_, 16, stride=32), :].astype(BF16)
-    mine = x * 2 + core
-    for step in range(1, 8):
+            into[target, r_] = update[pl.ds(target * 4 + r_, 16, stride=32), :].astype(BF16)
+
+    for step in (4, 5, 2, 3, 6, 7, 1):
         other = (mine + step) & 7
+        result_of(other, result_src)
         push(result_src.at[other], result_in.at[mine], RESULT, device((other >> 1) * 8 + y, zh, other & 1), rep)
     leaving.append((result_in.at[pl.ds(0, 7)], RESULT))
-    result_in[mine] = result_src[mine]
+    result_of(mine, result_in)
 
     arrived(final.at[pl.ds(0, 3)], FINAL)
     for half in range(2):

time: 73.9 us -> 73 us (0.988)
  Pallas kernels: 71.5 us -> 70.6 us
    pallas_call x1, Pallas kernels: 71.5 us -> 70.6 us  [shards(): pl.pallas_call(kernel, out_shape=(jax.ShapeDtypeStruct((ROWS * 8, 128), F...]
where the time goes in v9:
time: 73 us; the launch traced here: 72.9 us
  Pallas kernels  70.6 us (97%)
  local copies, waits for them, and re-layouts  1.67 us (2%)
    pallas_call x1, Pallas kernels, shards(): pl.pallas_call(kernel, out_shape=(jax.ShapeDtypeStruct((ROWS * 8, 128), F...  70.6 us
    unnamed x2, local copies, waits for them, and re-layouts  1.67 us

profile of v9, /device:TPU:1, one launch (start us, length us, event | category | flops | bytes accessed | tf_op | source)
XLA Modules:
  0.0 72.9 jit_solution(3032517959125640183)
XLA Ops:
  0.6 70.6 %shard_map.140 = (f32[2048,128]{1,0:T(8,128)S(1)}, f32[4,128,128]{2,1,0:T(8,128)S(1)}) custom-call(f32[2,512,256]{2,1,0:T(8,128)} %refs_0_.1, f32[4,128,128]{2,1,0:T(8,128)} %refs_1_.1, f32[1,256]{1,0:T(1,128)} %bitcast.14, bf16[256,1024]{1,0:T(8,128)(2,1)} %refs_3_.1, f32[1,128]{1,0:T(1,128)} %bitcast.17, bf16[8,128]{1,0:T(8,128)(2,1)} %bitcast.13, ...), custom_call_target="tpu_custom_call" | custom-call | tf_op jit(solution)/shard_map/pallas_call | solution.py:524
  71.2 1.0 %copy.18 = f32[256,4,256]{2,1,0:T(4,128)} copy(f32[256,4,256]{2,1,0:T(4,128)S(1)} %bitcast.11) | data formatting | bytes 2097152
  72.2 0.7 copy.19

commit v10 on v9

--- a/solution.py
+++ b/solution.py
@@ -214,16 +214,18 @@
             weights[s, which, :, y_] = powers.astype(BF16).reshape(4, 16, RES)
             denom[s, which, :, y_] = jnp.broadcast_to(1.0 / total, (64, 128)).reshape(4, 16, 128)
 
-    def row_finish(which):
+    def row_finish():
         for s in range(2):
-            attended = dot(weights[s, which].reshape(512, RES), values[s])
-            merged = merge_heads(attended, denom[s, which].reshape(512, 128)[:, :1])
-            gated = (merged * gates[s, which]).astype(BF16)
+            attended = dot(weights[s].reshape(1024, RES), values[s])
+            merged = merge_heads(attended, denom[s].reshape(1024, 128)[:, :1])
+            gated = (merged * gates[s].reshape(128, FEAT)).astype(BF16)
             change = dot(gated, wo_row[...])
-            for half in range(2):
-                staged[pl.ds(which * 4 + s * 2 + half, 64, stride=8), :] = (
-                    queries[s, which, half] + change[:, half * 128 : (half + 1) * 128]
-                )
+            for which in range(2):
+                for half in range(2):
+                    staged[pl.ds(which * 4 + s * 2 + half, 64, stride=8), :] = (
+                        queries[s, which, half]
+                        + change[which * 64 : (which + 1) * 64, half * 128 : (half + 1) * 128]
+                    )
 
     row_logits(0)
     for step in (1, 7, 2, 6, 3, 5, 4):
@@ -256,8 +258,7 @@
     row_softmax(own_arrived(0), core)
     lax.fori_loop(1, 8, both_queries, 0)
     row_softmax(other_arrived(7), 1 - core)
-    row_finish(core)
-    row_finish(1 - core)
+    row_finish()
     leaving.append((bias.at[0, pl.ds(0, 7), 0], BIAS_Y))
     leaving.append((bias.at[pl.ds(0, 3), :, 0], BIAS_X))
     leaving.append((bias.at[:, :, 0], BIAS_C))
@@ -311,7 +312,7 @@
         col_denom[rows, :] = jnp.broadcast_to(1.0 / total, (128, 128))
         return 0
 
-    lax.fori_loop(0, 16, col_softmax, 0, unroll=4)
+    lax.fori_loop(0, 16, col_softmax, 0, unroll=8)
     attended = dot(col_weights[...], col_values)
     merged = merge_heads(attended, col_denom[...][:, :1])
     gated = (merged * col_gates).astype(BF16)

time: 73 us -> 73 us (level)
  no operation moved by 1% of the time
where the time goes in v10:
time: 73 us; the launch traced here: 72.8 us
  Pallas kernels  70.5 us (97%)
  local copies, waits for them, and re-layouts  1.67 us (2%)
    pallas_call x1, Pallas kernels, shards(): pl.pallas_call(kernel, out_shape=(jax.ShapeDtypeStruct((ROWS * 8, 128), F...  70.5 us
    unnamed x2, local copies, waits for them, and re-layouts  1.67 us

profile of v10, /device:TPU:1, one launch (start us, length us, event | category | flops | bytes accessed | tf_op | source)
XLA Modules:
  0.0 72.8 jit_solution(12094795995889009701)
XLA Ops:
  0.6 70.5 %shard_map.140 = (f32[2048,128]{1,0:T(8,128)S(1)}, f32[4,128,128]{2,1,0:T(8,128)S(1)}) custom-call(f32[2,512,256]{2,1,0:T(8,128)} %refs_0_.1, f32[4,128,128]{2,1,0:T(8,128)} %refs_1_.1, f32[1,256]{1,0:T(1,128)} %bitcast.14, bf16[256,1024]{1,0:T(8,128)(2,1)} %refs_3_.1, f32[1,128]{1,0:T(1,128)} %bitcast.17, bf16[8,128]{1,0:T(8,128)(2,1)} %bitcast.13, ...), custom_call_target="tpu_custom_call" | custom-call | tf_op jit(solution)/shard_map/pallas_call | solution.py:525
  71.2 1.0 %copy.18 = f32[256,4,256]{2,1,0:T(4,128)} copy(f32[256,4,256]{2,1,0:T(4,128)S(1)} %bitcast.11) | data formatting | bytes 2097152
  72.1 0.7 copy.19
